TPU v7x, 512 devices: a whole 4x4x16 slice. The times are simulated.
512 devices in a mesh: gx: 8 (over y, core), yz: 64 (over x, z).
Axes of the slice: x: 4, y: 4, z: 16, core: 2. Of those that a mesh axis runs over, the one named last changes fastest.
Arguments:
- right_side: float32 [128, 2048, 128], P('gx', 'yz'), may hold values from -6 to 6
- coefficient: float32 [128, 2048, 128], P('gx', 'yz'), may hold values from 0.5 to 8
Outputs:
- solution: float32 [128, 2048, 128], P('gx', 'yz')
All inputs are finite; a program needn't handle non-finite values.
Results may differ from a plain program's by a relative error of at most 0.0001.
Values sent between devices are 32-bit elements; how exact they have to be, the bound alone decides.
A program may use at most 64 MiB of HBM per device.

v0:
```python
import jax
import jax.numpy as jnp
from jax import lax
from jax.sharding import PartitionSpec as P

LEVELS = 4
BITERS = 4


RELAXATION = 0.8


def padded_2(cells, sides, width):
    for axis, dim in sides:
        count = lax.axis_size(axis)
        ends = count - 1
        head = lax.slice_in_dim(cells, 0, width, axis=dim)
        tail = lax.slice_in_dim(cells, cells.shape[dim] - width, cells.shape[dim], axis=dim)
        cells = jnp.concatenate(
            [
                lax.ppermute(tail, axis, [(i, (i + 1) % count) for i in range(ends)]),
                cells,
                lax.ppermute(head, axis, [((i + 1) % count, i) for i in range(ends)]),
            ],
            axis=dim,
        )
    return cells


def neighbours(padded):
    return [
        padded[2:, 1:-1, 1:-1],
        padded[:-2, 1:-1, 1:-1],
        padded[1:-1, 2:, 1:-1],
        padded[1:-1, :-2, 1:-1],
        padded[1:-1, 1:-1, 2:],
        padded[1:-1, 1:-1, :-2],
    ]


def face_weights(padded):
    centre = padded[1:-1, 1:-1, 1:-1]
    return [0.5 * (centre + other) for other in neighbours(padded)]


def diagonal_of(face_list, level_scale):
    summed = face_list[0]
    for weight in face_list[1:]:
        summed = summed + weight
    return level_scale * summed


def operate(padded, face_list, level_scale):
    centre = padded[1:-1, 1:-1, 1:-1]
    others = neighbours(padded)
    summed = face_list[0] * (centre - others[0])
    for position in range(1, 6):
        summed = summed + face_list[position] * (centre - others[position])
    return level_scale * summed


def restrict(values):
    return values.reshape(
        values.shape[0] // 2, 2, values.shape[1] // 2, 2, values.shape[2] // 2, 2
    ).mean(axis=(1, 3, 5))


def prolong(values):
    return jnp.repeat(jnp.repeat(jnp.repeat(values, 2, 0), 2, 1), 2, 2)


def padded_box(values):
    framed = padded_2(values, (("gx", 0), ("yz", 1)), 1)
    return jnp.pad(framed, ((0, 0), (0, 0), (1, 1)))


def padded_slab(values):
    framed = padded_2(values, (("gx", 0),), 1)
    return jnp.pad(framed, ((0, 0), (1, 1), (1, 1)))


def stabilized_solve(source, weight):
    level_scale = 0.25**LEVELS
    face_list = face_weights(padded_slab(weight))

    def apply_op(values):
        return operate(padded_slab(values), face_list, level_scale)

    answer = jnp.zeros_like(source)
    residual = source
    rho_now = lax.psum(jnp.sum(source * residual), "gx")
    rho_prev = rho_now
    direction = residual
    applied = jnp.zeros_like(source)
    step_alpha = jnp.float32(1.0)
    step_omega = jnp.float32(1.0)
    for turn_index in range(BITERS):
        if turn_index > 0:
            beta_factor = rho_now / rho_prev * (step_alpha / step_omega)
            direction = residual + beta_factor * (direction - step_omega * applied)
        applied = apply_op(direction)
        step_alpha = rho_now / lax.psum(jnp.sum(source * applied), "gx")
        middle = residual - step_alpha * applied
        bent_image = apply_op(middle)
        pair_sums = lax.psum((jnp.sum(bent_image * middle), jnp.sum(bent_image * bent_image)), "gx")
        step_omega = pair_sums[0] / pair_sums[1]
        answer = answer + step_alpha * direction + step_omega * middle
        residual = middle - step_omega * bent_image
        if turn_index + 1 < BITERS:
            rho_prev = rho_now
            rho_now = lax.psum(jnp.sum(source * residual), "gx")
    return answer


def per_device(right_side, coefficient):
    source = right_side
    weight = coefficient
    stored = []
    for level_index in range(LEVELS):
        merged = False
        level_scale = 0.25**level_index
        padder = padded_box
        face_list = face_weights(padder(weight))
        diagonal = diagonal_of(face_list, level_scale)
        iterate = RELAXATION * source / diagonal
        iterate = (
            iterate
            + RELAXATION * (source - operate(padder(iterate), face_list, level_scale)) / diagonal
        )
        residual = source - operate(padder(iterate), face_list, level_scale)
        stored.append((source, iterate, face_list, diagonal, merged))
        if level_index == LEVELS - 1:
            residual, weight = (
                lax.all_gather(residual, "yz", axis=1, tiled=True),
                lax.all_gather(weight, "yz", axis=1, tiled=True),
            )
        source = restrict(residual)
        weight = restrict(weight)
    correction = stabilized_solve(source, weight)
    for level_index in reversed(range(LEVELS)):
        source, iterate, face_list, diagonal, merged = stored[level_index]
        level_scale = 0.25**level_index
        padder = padded_box
        widened = prolong(correction)
        if widened.shape[1] != iterate.shape[1]:
            own_rows = iterate.shape[1]
            widened = lax.dynamic_slice_in_dim(
                widened, lax.axis_index("yz") * own_rows, own_rows, 1
            )
        iterate = iterate + widened
        iterate = (
            iterate
            + RELAXATION * (source - operate(padder(iterate), face_list, level_scale)) / diagonal
        )
        correction = iterate
    return correction


def solution(mesh):
    return jax.shard_map(
        per_device,
        mesh=mesh,
        in_specs=(P("gx", "yz", None), P("gx", "yz", None)),
        out_specs=P("gx", "yz", None),
        check_vma=False,
    )
```

profile of v0, /device:TPU:1, one launch (start us, length us, event | category | flops | bytes accessed | tf_op | source)
XLA Modules:
  0.0 709.4 jit_solution(8978130539700495041)
XLA Ops:
  0.7 4.6 collective-permute-start.1
  5.3 5.5 collective-permute-start
  13.2 4.1 collective-permute-start.3
  17.3 18.8 %reshape.93 = f32[8,2,16,2,64,2]{5,4,3,2,1,0:T(8,128)} reshape(f32[16,32,128]{2,1,0:T(8,128)} %param.3) | data formatting | bytes 524288 | tf_op jit(solution)/shard_map/reshape | solution.py:63
  36.1 7.0 reduce_sum.231
  46.5 2.9 collective-permute-start.5
  52.2 4.6 collective-permute-start.7
  59.3 4.8 collective-permute-start.13
  72.6 3.6 collective-permute-start.9
  78.3 4.0 collective-permute-start.15
  83.7 4.0 collective-permute-start.11
  90.4 18.1 %reshape.92 = f32[8,2,16,2,64,2]{5,4,3,2,1,0:T(8,128)} reshape(f32[16,32,128]{2,1,0:T(8,128)S(1)} %fusion.22) | data formatting | bytes 524288 | tf_op jit(solution)/shard_map/reshape | solution.py:63
  108.4 7.0 reduce_sum.230
  118.6 3.3 collective-permute-start.17
  124.0 5.1 collective-permute-start.19
  131.0 4.5 collective-permute-start.25
  139.3 3.6 collective-permute-start.21
  144.3 5.2 collective-permute-start.27
  150.9 5.4 collective-permute-start.23
  158.7 3.0 reshape.94
  165.4 3.6 collective-permute-start.29
  171.1 5.6 collective-permute-start.31
  178.7 4.5 collective-permute-start.37
  186.1 3.6 collective-permute-start.33
  191.1 5.2 collective-permute-start.39
  197.6 5.2 collective-permute-start.35
  207.4 3.6 collective-permute-start.41
  213.1 5.5 collective-permute-start.43
  218.6 83.0 %all_gather.7 = f32[2,256,16]{2,0,1:T(2,128)S(1)} all-gather(f32[2,4,16]{2,0,1:T(2,128)S(1)} %copy.324), channel_id=1, replica_groups=mesh['gx'=8,'yz'=64] {'yz'}, dimensions={1}, use_global_device_ids=true | all-gather | bytes 33280 | tf_op jit(solution)/shard_map/all_gather | solution.py:135
  301.8 20.9 %collective-permute-start.44 = (f32[1,4,16]{2,1,0:T(4,128)S(1)}, f32[1,4,16]{2,1,0:T(4,128)S(1)}, u32[]{:S(2)}, u32[]{:S(2)}) collective-permute-start(f32[1,4,16]{2,1,0:T(4,128)S(1)} %get-tuple-element.118), channel_id=1, source_target_pairs={{64,0},{128,64},{192,128},{256,192},{320,256},{384,320},{448,384},... | collective-permute-start | bytes 776 | tf_op jit(solution)/shard_map/ppermute | solution.py:23
  322.7 4.9 collective-permute-start.45
  330.6 4.0 collective-permute-start.47
  336.5 3.8 collective-permute-start.50
  340.5 62.1 %all_gather.6 = f32[2,256,16]{2,0,1:T(2,128)S(1)} all-gather(f32[2,4,16]{2,0,1:T(2,128)S(1)} %copy.321), channel_id=1, replica_groups=mesh['gx'=8,'yz'=64] {'yz'}, dimensions={1}, use_global_device_ids=true | all-gather | bytes 33280 | tf_op jit(solution)/shard_map/all_gather | solution.py:134
  404.9 19.8 %collective-permute-start.49 = (f32[1,128,8]{1,2,0:T(8,128)S(1)}, f32[1,128,8]{1,2,0:T(8,128)S(1)}, u32[]{:S(2)}, u32[]{:S(2)}) collective-permute-start(f32[1,128,8]{1,2,0:T(8,128)S(1)} %get-tuple-element.116), channel_id=1, source_target_pairs={{64,0},{128,64},{192,128},{256,192},{320,256},{384,320},{448,384},... | collective-permute-start | bytes 12296 | tf_op jit(solution)/shard_map/ppermute | solution.py:23
  424.7 3.8 collective-permute-start.51
  430.0 13.6 %all-reduce.29 = (f32[]{:T(128)}, f32[]{:T(128)}) all-reduce(f32[]{:T(128)} %get-tuple-element.115, f32[]{:T(128)} %get-tuple-element.36), channel_id=1, replica_groups=mesh['gx'=8,'yz'=64] {'gx'}, use_global_device_ids=true, to_apply=%region_9.10 | all-reduce | flops 2 | bytes 16 | tf_op jit(solution)/shard_map/psum | solution.py:91
  445.0 3.6 collective-permute-start.52
  452.5 12.6 %all-reduce.28 = (f32[]{:T(128)}, f32[]{:T(128)}) all-reduce(f32[]{:T(128)} %get-tuple-element.12, f32[]{:T(128)} %get-tuple-element.11), channel_id=1, replica_groups=mesh['gx'=8,'yz'=64] {'gx'}, use_global_device_ids=true, to_apply=%region_15.16 | all-reduce | flops 2 | bytes 16 | tf_op jit(solution)/shard_map/psum | solution.py:105
  469.5 13.2 %psum.116 = f32[]{:T(128)} all-reduce(f32[]{:T(128)} %multiply_reduce_fusion.11), channel_id=1, replica_groups=mesh['gx'=8,'yz'=64] {'gx'}, use_global_device_ids=true, to_apply=%region_19.20 | all-reduce | flops 1 | bytes 8 | tf_op jit(solution)/shard_map/psum | solution.py:111
  486.6 3.0 collective-permute-start.55
  491.1 11.9 %psum.117 = f32[]{:T(128)} all-reduce(f32[]{:T(128)} %get-tuple-element.33), channel_id=1, replica_groups=mesh['gx'=8,'yz'=64] {'gx'}, use_global_device_ids=true, to_apply=%region_21.22 | all-reduce | flops 1 | bytes 8 | tf_op jit(solution)/shard_map/psum | solution.py:102
  504.2 3.6 collective-permute-start.56
  511.7 12.6 %all-reduce.27 = (f32[]{:T(128)}, f32[]{:T(128)}) all-reduce(f32[]{:T(128)} %get-tuple-element.10, f32[]{:T(128)} %get-tuple-element.9), channel_id=1, replica_groups=mesh['gx'=8,'yz'=64] {'gx'}, use_global_device_ids=true, to_apply=%region_23.24 | all-reduce | flops 2 | bytes 16 | tf_op jit(solution)/shard_map/psum | solution.py:105
  528.7 13.4 %psum.120 = f32[]{:T(128)} all-reduce(f32[]{:T(128)} %get-tuple-element.30), channel_id=1, replica_groups=mesh['gx'=8,'yz'=64] {'gx'}, use_global_device_ids=true, to_apply=%region_27.28 | all-reduce | flops 1 | bytes 8 | tf_op jit(solution)/shard_map/psum | solution.py:111
  546.0 3.0 collective-permute-start.59
  550.5 11.9 %psum.121 = f32[]{:T(128)} all-reduce(f32[]{:T(128)} %get-tuple-element.28), channel_id=1, replica_groups=mesh['gx'=8,'yz'=64] {'gx'}, use_global_device_ids=true, to_apply=%region_29.30 | all-reduce | flops 1 | bytes 8 | tf_op jit(solution)/shard_map/psum | solution.py:102
  563.8 3.6 collective-permute-start.60
  571.3 12.6 %all-reduce.26 = (f32[]{:T(128)}, f32[]{:T(128)}) all-reduce(f32[]{:T(128)} %get-tuple-element.8, f32[]{:T(128)} %get-tuple-element.7), channel_id=1, replica_groups=mesh['gx'=8,'yz'=64] {'gx'}, use_global_device_ids=true, to_apply=%region_31.32 | all-reduce | flops 2 | bytes 16 | tf_op jit(solution)/shard_map/psum | solution.py:105
  588.4 13.4 %psum.124 = f32[]{:T(128)} all-reduce(f32[]{:T(128)} %get-tuple-element.25), channel_id=1, replica_groups=mesh['gx'=8,'yz'=64] {'gx'}, use_global_device_ids=true, to_apply=%region_35.36 | all-reduce | flops 1 | bytes 8 | tf_op jit(solution)/shard_map/psum | solution.py:111
  605.8 3.0 collective-permute-start.63
  610.4 11.9 %psum.125 = f32[]{:T(128)} all-reduce(f32[]{:T(128)} %get-tuple-element.23), channel_id=1, replica_groups=mesh['gx'=8,'yz'=64] {'gx'}, use_global_device_ids=true, to_apply=%region_37.38 | all-reduce | flops 1 | bytes 8 | tf_op jit(solution)/shard_map/psum | solution.py:102
  623.6 3.6 collective-permute-start.64
  631.1 12.6 %all-reduce.25 = (f32[]{:T(128)}, f32[]{:T(128)}) all-reduce(f32[]{:T(128)} %get-tuple-element.6, f32[]{:T(128)} %get-tuple-element.5), channel_id=1, replica_groups=mesh['gx'=8,'yz'=64] {'gx'}, use_global_device_ids=true, to_apply=%region_39.40 | all-reduce | flops 2 | bytes 16 | tf_op jit(solution)/shard_map/psum | solution.py:105
  645.5 2.9 collective-permute-start.66
  648.3 2.7 collective-permute-start.67
  653.0 4.0 collective-permute-start.69
  658.2 2.8 collective-permute-start.70
  661.0 4.4 collective-permute-start.71
  667.4 4.5 collective-permute-start.73
  676.1 5.0 collective-permute-start.75
  683.3 4.5 collective-permute-start.77
  694.4 5.0 collective-permute-start.79
  701.7 4.5 collective-permute-start.81
  (306 shorter events, 123.5 us)
Async XLA Ops:
  0.7 10.1 %collective-permute-start.1 = (f32[1,32,128]{2,1,0:T(8,128)S(1)}, f32[1,32,128]{2,1,0:T(8,128)S(1)}, u32[]{:S(2)}, u32[]{:S(2)}) collective-permute-start(f32[1,32,128]{2,1,0:T(8,128)S(1)} %get-tuple-element.71), channel_id=1, source_target_pairs={{0,64},{64,128},{128,192},{192,256},{256,320},{320,384},{384,448},... | collective-permute-start | bytes 49160 | tf_op jit(solution)/shard_map/ppermute | solution.py:21
  5.3 6.5 collective-permute-start
  11.9 31.3 %collective-permute-start.2 = (f32[18,1,128]{2,1,0:T(1,128)S(1)}, f32[18,1,128]{2,1,0:T(1,128)S(1)}, u32[]{:S(2)}, u32[]{:S(2)}) collective-permute-start(f32[18,1,128]{2,1,0:T(1,128)S(1)} %get-tuple-element.64), channel_id=1, source_target_pairs={{1,0},{2,1},{3,2},{4,3},{5,4},{6,5},{7,6},{8,7},{9,8},{10,9},{11,1... | collective-permute-start | bytes 27656 | tf_op jit(solution)/shard_map/ppermute | solution.py:23
  13.2 30.0 %collective-permute-start.3 = (f32[18,1,128]{2,1,0:T(1,128)S(1)}, f32[18,1,128]{2,1,0:T(1,128)S(1)}, u32[]{:S(2)}, u32[]{:S(2)}) collective-permute-start(f32[18,1,128]{2,1,0:T(1,128)S(1)} %get-tuple-element.63), channel_id=1, source_target_pairs={{0,1},{1,2},{2,3},{3,4},{4,5},{5,6},{6,7},{7,8},{8,9},{9,10},{10,1... | collective-permute-start | bytes 27656 | tf_op jit(solution)/shard_map/ppermute | solution.py:21
  43.9 5.6 collective-permute-start.4
  50.9 16.2 %collective-permute-start.6 = (f32[18,1,128]{2,1,0:T(1,128)}, f32[18,1,128]{2,1,0:T(1,128)}, u32[]{:S(2)}, u32[]{:S(2)}) collective-permute-start(f32[18,1,128]{2,1,0:T(1,128)} %get-tuple-element.62), channel_id=1, source_target_pairs={{1,0},{2,1},{3,2},{4,3},{5,4},{6,5},{7,6},{8,7},{9,8},{10,9},{11,1... | collective-permute-start | bytes 27656 | tf_op jit(solution)/shard_map/ppermute | solution.py:23
  52.2 14.9 %collective-permute-start.7 = (f32[18,1,128]{2,1,0:T(1,128)}, f32[18,1,128]{2,1,0:T(1,128)}, u32[]{:S(2)}, u32[]{:S(2)}) collective-permute-start(f32[18,1,128]{2,1,0:T(1,128)} %get-tuple-element.61), channel_id=1, source_target_pairs={{0,1},{1,2},{2,3},{3,4},{4,5},{5,6},{6,7},{7,8},{8,9},{9,10},{10,1... | collective-permute-start | bytes 27656 | tf_op jit(solution)/shard_map/ppermute | solution.py:21
  57.4 18.9 %collective-permute-start.12 = (f32[1,16,64]{2,1,0:T(8,128)}, f32[1,16,64]{2,1,0:T(8,128)}, u32[]{:S(2)}, u32[]{:S(2)}) collective-permute-start(f32[1,16,64]{2,1,0:T(8,128)} %get-tuple-element.88), channel_id=1, source_target_pairs={{64,0},{128,64},{192,128},{256,192},{320,256},{384,320},{448,384},... | collective-permute-start | bytes 12296 | tf_op jit(solution)/shard_map/ppermute | solution.py:23
  59.3 17.0 %collective-permute-start.13 = (f32[1,16,64]{2,1,0:T(8,128)}, f32[1,16,64]{2,1,0:T(8,128)}, u32[]{:S(2)}, u32[]{:S(2)}) collective-permute-start(f32[1,16,64]{2,1,0:T(8,128)} %get-tuple-element.87), channel_id=1, source_target_pairs={{0,64},{64,128},{128,192},{192,256},{256,320},{320,384},{384,448},... | collective-permute-start | bytes 12296 | tf_op jit(solution)/shard_map/ppermute | solution.py:21
  70.7 11.6 %collective-permute-start.8 = (f32[1,32,128]{2,1,0:T(8,128)S(1)}, f32[1,32,128]{2,1,0:T(8,128)S(1)}, u32[]{:S(2)}, u32[]{:S(2)}) collective-permute-start(f32[1,32,128]{2,1,0:T(8,128)S(1)} %get-tuple-element.68), channel_id=1, source_target_pairs={{64,0},{128,64},{192,128},{256,192},{320,256},{384,320},{448,384},... | collective-permute-start | bytes 49160 | tf_op jit(solution)/shard_map/ppermute | solution.py:23
  72.6 9.7 %collective-permute-start.9 = (f32[1,32,128]{2,1,0:T(8,128)S(1)}, f32[1,32,128]{2,1,0:T(8,128)S(1)}, u32[]{:S(2)}, u32[]{:S(2)}) collective-permute-start(f32[1,32,128]{2,1,0:T(8,128)S(1)} %get-tuple-element.67), channel_id=1, source_target_pairs={{0,64},{64,128},{128,192},{192,256},{256,320},{320,384},{384,448},... | collective-permute-start | bytes 49160 | tf_op jit(solution)/shard_map/ppermute | solution.py:21
  77.0 10.6 %collective-permute-start.14 = (f32[10,1,64]{2,1,0:T(1,128)S(1)}, f32[10,1,64]{2,1,0:T(1,128)S(1)}, u32[]{:S(2)}, u32[]{:S(2)}) collective-permute-start(f32[10,1,64]{2,1,0:T(1,128)S(1)} %get-tuple-element.80), channel_id=1, source_target_pairs={{1,0},{2,1},{3,2},{4,3},{5,4},{6,5},{7,6},{8,7},{9,8},{10,9},{11,1... | collective-permute-start | bytes 7688 | tf_op jit(solution)/shard_map/ppermute | solution.py:23
  78.3 9.4 %collective-permute-start.15 = (f32[10,1,64]{2,1,0:T(1,128)S(1)}, f32[10,1,64]{2,1,0:T(1,128)S(1)}, u32[]{:S(2)}, u32[]{:S(2)}) collective-permute-start(f32[10,1,64]{2,1,0:T(1,128)S(1)} %get-tuple-element.79), channel_id=1, source_target_pairs={{0,1},{1,2},{2,3},{3,4},{4,5},{5,6},{6,7},{7,8},{8,9},{9,10},{10,1... | collective-permute-start | bytes 7688 | tf_op jit(solution)/shard_map/ppermute | solution.py:21
  82.3 6.2 collective-permute-start.10
  116.3 5.6 collective-permute-start.16
  122.7 13.7 %collective-permute-start.18 = (f32[10,1,64]{2,1,0:T(1,128)S(1)}, f32[10,1,64]{2,1,0:T(1,128)S(1)}, u32[]{:S(2)}, u32[]{:S(2)}) collective-permute-start(f32[10,1,64]{2,1,0:T(1,128)S(1)} %get-tuple-element.78), channel_id=1, source_target_pairs={{1,0},{2,1},{3,2},{4,3},{5,4},{6,5},{7,6},{8,7},{9,8},{10,9},{11,1... | collective-permute-start | bytes 7688 | tf_op jit(solution)/shard_map/ppermute | solution.py:23
  124.0 12.4 %collective-permute-start.19 = (f32[10,1,64]{2,1,0:T(1,128)S(1)}, f32[10,1,64]{2,1,0:T(1,128)S(1)}, u32[]{:S(2)}, u32[]{:S(2)}) collective-permute-start(f32[10,1,64]{2,1,0:T(1,128)S(1)} %get-tuple-element.77), channel_id=1, source_target_pairs={{0,1},{1,2},{2,3},{3,4},{4,5},{5,6},{6,7},{7,8},{8,9},{9,10},{10,1... | collective-permute-start | bytes 7688 | tf_op jit(solution)/shard_map/ppermute | solution.py:21
  129.1 13.9 %collective-permute-start.24 = (f32[1,8,32]{2,1,0:T(8,128)S(1)}, f32[1,8,32]{2,1,0:T(8,128)S(1)}, u32[]{:S(2)}, u32[]{:S(2)}) collective-permute-start(f32[1,8,32]{2,1,0:T(8,128)S(1)} %get-tuple-element.104), channel_id=1, source_target_pairs={{64,0},{128,64},{192,128},{256,192},{320,256},{384,320},{448,384},... | collective-permute-start | bytes 3080 | tf_op jit(solution)/shard_map/ppermute | solution.py:23
  131.0 12.0 %collective-permute-start.25 = (f32[1,8,32]{2,1,0:T(8,128)S(1)}, f32[1,8,32]{2,1,0:T(8,128)S(1)}, u32[]{:S(2)}, u32[]{:S(2)}) collective-permute-start(f32[1,8,32]{2,1,0:T(8,128)S(1)} %get-tuple-element.103), channel_id=1, source_target_pairs={{0,64},{64,128},{128,192},{192,256},{256,320},{320,384},{384,448},... | collective-permute-start | bytes 3080 | tf_op jit(solution)/shard_map/ppermute | solution.py:21
  137.4 12.1 %collective-permute-start.20 = (f32[1,16,64]{2,1,0:T(8,128)S(1)}, f32[1,16,64]{2,1,0:T(8,128)S(1)}, u32[]{:S(2)}, u32[]{:S(2)}) collective-permute-start(f32[1,16,64]{2,1,0:T(8,128)S(1)} %get-tuple-element.84), channel_id=1, source_target_pairs={{64,0},{128,64},{192,128},{256,192},{320,256},{384,320},{448,384},... | collective-permute-start | bytes 12296 | tf_op jit(solution)/shard_map/ppermute | solution.py:23
  139.3 10.2 %collective-permute-start.21 = (f32[1,16,64]{2,1,0:T(8,128)S(1)}, f32[1,16,64]{2,1,0:T(8,128)S(1)}, u32[]{:S(2)}, u32[]{:S(2)}) collective-permute-start(f32[1,16,64]{2,1,0:T(8,128)S(1)} %get-tuple-element.83), channel_id=1, source_target_pairs={{0,64},{64,128},{128,192},{192,256},{256,320},{320,384},{384,448},... | collective-permute-start | bytes 12296 | tf_op jit(solution)/shard_map/ppermute | solution.py:21
  143.0 13.2 %collective-permute-start.26 = (f32[6,1,32]{2,1,0:T(1,128)S(1)}, f32[6,1,32]{2,1,0:T(1,128)S(1)}, u32[]{:S(2)}, u32[]{:S(2)}) collective-permute-start(f32[6,1,32]{2,1,0:T(1,128)S(1)} %get-tuple-element.96), channel_id=1, source_target_pairs={{1,0},{2,1},{3,2},{4,3},{5,4},{6,5},{7,6},{8,7},{9,8},{10,9},{11,1... | collective-permute-start | bytes 2312 | tf_op jit(solution)/shard_map/ppermute | solution.py:23
  144.3 12.0 %collective-permute-start.27 = (f32[6,1,32]{2,1,0:T(1,128)S(1)}, f32[6,1,32]{2,1,0:T(1,128)S(1)}, u32[]{:S(2)}, u32[]{:S(2)}) collective-permute-start(f32[6,1,32]{2,1,0:T(1,128)S(1)} %get-tuple-element.95), channel_id=1, source_target_pairs={{0,1},{1,2},{2,3},{3,4},{4,5},{5,6},{6,7},{7,8},{8,9},{9,10},{10,1... | collective-permute-start | bytes 2312 | tf_op jit(solution)/shard_map/ppermute | solution.py:21
  149.6 7.5 %collective-permute-start.22 = (f32[10,1,64]{2,1,0:T(1,128)S(1)}, f32[10,1,64]{2,1,0:T(1,128)S(1)}, u32[]{:S(2)}, u32[]{:S(2)}) collective-permute-start(f32[10,1,64]{2,1,0:T(1,128)S(1)} %get-tuple-element.76), channel_id=1, source_target_pairs={{1,0},{2,1},{3,2},{4,3},{5,4},{6,5},{7,6},{8,7},{9,8},{10,9},{11,1... | collective-permute-start | bytes 7688 | tf_op jit(solution)/shard_map/ppermute | solution.py:23
  150.9 6.2 collective-permute-start.23
  163.5 6.3 collective-permute-start.28
  169.8 13.4 %collective-permute-start.30 = (f32[6,1,32]{2,1,0:T(1,128)S(1)}, f32[6,1,32]{2,1,0:T(1,128)S(1)}, u32[]{:S(2)}, u32[]{:S(2)}) collective-permute-start(f32[6,1,32]{2,1,0:T(1,128)S(1)} %get-tuple-element.94), channel_id=1, source_target_pairs={{1,0},{2,1},{3,2},{4,3},{5,4},{6,5},{7,6},{8,7},{9,8},{10,9},{11,1... | collective-permute-start | bytes 2312 | tf_op jit(solution)/shard_map/ppermute | solution.py:23
  171.1 12.1 %collective-permute-start.31 = (f32[6,1,32]{2,1,0:T(1,128)S(1)}, f32[6,1,32]{2,1,0:T(1,128)S(1)}, u32[]{:S(2)}, u32[]{:S(2)}) collective-permute-start(f32[6,1,32]{2,1,0:T(1,128)S(1)} %get-tuple-element.93), channel_id=1, source_target_pairs={{0,1},{1,2},{2,3},{3,4},{4,5},{5,6},{6,7},{7,8},{8,9},{9,10},{10,1... | collective-permute-start | bytes 2312 | tf_op jit(solution)/shard_map/ppermute | solution.py:21
  176.8 12.9 %collective-permute-start.36 = (f32[1,4,16]{2,1,0:T(4,128)S(1)}, f32[1,4,16]{2,1,0:T(4,128)S(1)}, u32[]{:S(2)}, u32[]{:S(2)}) collective-permute-start(f32[1,4,16]{2,1,0:T(4,128)S(1)} %get-tuple-element.122), channel_id=1, source_target_pairs={{64,0},{128,64},{192,128},{256,192},{320,256},{384,320},{448,384},... | collective-permute-start | bytes 776 | tf_op jit(solution)/shard_map/ppermute | solution.py:23
  178.7 11.0 %collective-permute-start.37 = (f32[1,4,16]{2,1,0:T(4,128)S(1)}, f32[1,4,16]{2,1,0:T(4,128)S(1)}, u32[]{:S(2)}, u32[]{:S(2)}) collective-permute-start(f32[1,4,16]{2,1,0:T(4,128)S(1)} %get-tuple-element.121), channel_id=1, source_target_pairs={{0,64},{64,128},{128,192},{192,256},{256,320},{320,384},{384,448},... | collective-permute-start | bytes 776 | tf_op jit(solution)/shard_map/ppermute | solution.py:21
  184.1 12.1 %collective-permute-start.32 = (f32[1,8,32]{2,1,0:T(8,128)S(1)}, f32[1,8,32]{2,1,0:T(8,128)S(1)}, u32[]{:S(2)}, u32[]{:S(2)}) collective-permute-start(f32[1,8,32]{2,1,0:T(8,128)S(1)} %get-tuple-element.100), channel_id=1, source_target_pairs={{64,0},{128,64},{192,128},{256,192},{320,256},{384,320},{448,384},... | collective-permute-start | bytes 3080 | tf_op jit(solution)/shard_map/ppermute | solution.py:23
  186.1 10.2 %collective-permute-start.33 = (f32[1,8,32]{2,1,0:T(8,128)S(1)}, f32[1,8,32]{2,1,0:T(8,128)S(1)}, u32[]{:S(2)}, u32[]{:S(2)}) collective-permute-start(f32[1,8,32]{2,1,0:T(8,128)S(1)} %get-tuple-element.99), channel_id=1, source_target_pairs={{0,64},{64,128},{128,192},{192,256},{256,320},{320,384},{384,448},... | collective-permute-start | bytes 3080 | tf_op jit(solution)/shard_map/ppermute | solution.py:21
  189.8 13.1 %collective-permute-start.38 = (f32[4,1,16]{2,1,0:T(1,128)S(1)}, f32[4,1,16]{2,1,0:T(1,128)S(1)}, u32[]{:S(2)}, u32[]{:S(2)}) collective-permute-start(f32[4,1,16]{2,1,0:T(1,128)S(1)} %get-tuple-element.112), channel_id=1, source_target_pairs={{1,0},{2,1},{3,2},{4,3},{5,4},{6,5},{7,6},{8,7},{9,8},{10,9},{11,1... | collective-permute-start | bytes 776 | tf_op jit(solution)/shard_map/ppermute | solution.py:23
  191.1 11.8 %collective-permute-start.39 = (f32[4,1,16]{2,1,0:T(1,128)S(1)}, f32[4,1,16]{2,1,0:T(1,128)S(1)}, u32[]{:S(2)}, u32[]{:S(2)}) collective-permute-start(f32[4,1,16]{2,1,0:T(1,128)S(1)} %get-tuple-element.111), channel_id=1, source_target_pairs={{0,1},{1,2},{2,3},{3,4},{4,5},{5,6},{6,7},{7,8},{8,9},{9,10},{10,1... | collective-permute-start | bytes 776 | tf_op jit(solution)/shard_map/ppermute | solution.py:21
  196.3 6.6 collective-permute-start.34
  197.6 5.9 collective-permute-start.35
  205.5 5.6 collective-permute-start.40
  211.8 89.8 %collective-permute-start.42 = (f32[4,1,16]{2,1,0:T(1,128)S(1)}, f32[4,1,16]{2,1,0:T(1,128)S(1)}, u32[]{:S(2)}, u32[]{:S(2)}) collective-permute-start(f32[4,1,16]{2,1,0:T(1,128)S(1)} %get-tuple-element.110), channel_id=1, source_target_pairs={{1,0},{2,1},{3,2},{4,3},{5,4},{6,5},{7,6},{8,7},{9,8},{10,9},{11,1... | collective-permute-start | bytes 776 | tf_op jit(solution)/shard_map/ppermute | solution.py:23
  213.1 88.5 %collective-permute-start.43 = (f32[4,1,16]{2,1,0:T(1,128)S(1)}, f32[4,1,16]{2,1,0:T(1,128)S(1)}, u32[]{:S(2)}, u32[]{:S(2)}) collective-permute-start(f32[4,1,16]{2,1,0:T(1,128)S(1)} %get-tuple-element.109), channel_id=1, source_target_pairs={{0,1},{1,2},{2,3},{3,4},{4,5},{5,6},{6,7},{7,8},{8,9},{9,10},{10,1... | collective-permute-start | bytes 776 | tf_op jit(solution)/shard_map/ppermute | solution.py:21
  301.8 27.5 %collective-permute-start.44 = (f32[1,4,16]{2,1,0:T(4,128)S(1)}, f32[1,4,16]{2,1,0:T(4,128)S(1)}, u32[]{:S(2)}, u32[]{:S(2)}) collective-permute-start(f32[1,4,16]{2,1,0:T(4,128)S(1)} %get-tuple-element.118), channel_id=1, source_target_pairs={{64,0},{128,64},{192,128},{256,192},{320,256},{384,320},{448,384},... | collective-permute-start | bytes 776 | tf_op jit(solution)/shard_map/ppermute | solution.py:23
  322.7 6.6 collective-permute-start.45
  329.3 11.0 %collective-permute-start.46 = (f32[4,1,16]{2,1,0:T(1,128)S(1)}, f32[4,1,16]{2,1,0:T(1,128)S(1)}, u32[]{:S(2)}, u32[]{:S(2)}) collective-permute-start(f32[4,1,16]{2,1,0:T(1,128)S(1)} %get-tuple-element.108), channel_id=1, source_target_pairs={{1,0},{2,1},{3,2},{4,3},{5,4},{6,5},{7,6},{8,7},{9,8},{10,9},{11,1... | collective-permute-start | bytes 776 | tf_op jit(solution)/shard_map/ppermute | solution.py:23
  330.6 9.8 %collective-permute-start.47 = (f32[4,1,16]{2,1,0:T(1,128)S(1)}, f32[4,1,16]{2,1,0:T(1,128)S(1)}, u32[]{:S(2)}, u32[]{:S(2)}) collective-permute-start(f32[4,1,16]{2,1,0:T(1,128)S(1)} %get-tuple-element.107), channel_id=1, source_target_pairs={{0,1},{1,2},{2,3},{3,4},{4,5},{5,6},{6,7},{7,8},{8,9},{9,10},{10,1... | collective-permute-start | bytes 776 | tf_op jit(solution)/shard_map/ppermute | solution.py:21
  334.6 93.9 %collective-permute-start.48 = (f32[1,128,8]{1,2,0:T(8,128)S(1)}, f32[1,128,8]{1,2,0:T(8,128)S(1)}, u32[]{:S(2)}, u32[]{:S(2)}) collective-permute-start(f32[1,128,8]{1,2,0:T(8,128)S(1)} %multiply_bitcast_fusion), channel_id=1, source_target_pairs={{64,0},{128,64},{192,128},{256,192},{320,256},{384,320},{448,384},... | collective-permute-start | bytes 12296 | tf_op jit(solution)/shard_map/ppermute | solution.py:23
  336.5 92.0 %collective-permute-start.50 = (f32[1,128,8]{1,2,0:T(8,128)S(1)}, f32[1,128,8]{1,2,0:T(8,128)S(1)}, u32[]{:S(2)}, u32[]{:S(2)}) collective-permute-start(f32[1,128,8]{1,2,0:T(8,128)S(1)} %multiply_bitcast_fusion), channel_id=1, source_target_pairs={{0,64},{64,128},{128,192},{192,256},{256,320},{320,384},{384,448},... | collective-permute-start | bytes 12296 | tf_op jit(solution)/shard_map/ppermute | solution.py:21
  404.9 23.7 %collective-permute-start.49 = (f32[1,128,8]{1,2,0:T(8,128)S(1)}, f32[1,128,8]{1,2,0:T(8,128)S(1)}, u32[]{:S(2)}, u32[]{:S(2)}) collective-permute-start(f32[1,128,8]{1,2,0:T(8,128)S(1)} %get-tuple-element.116), channel_id=1, source_target_pairs={{64,0},{128,64},{192,128},{256,192},{320,256},{384,320},{448,384},... | collective-permute-start | bytes 12296 | tf_op jit(solution)/shard_map/ppermute | solution.py:23
  445.0 5.6 collective-permute-start.52
  484.0 5.6 collective-permute-start.54
  504.2 5.6 collective-permute-start.56
  543.4 5.6 collective-permute-start.58
  563.8 5.6 collective-permute-start.60
  603.2 5.6 collective-permute-start.62
  623.6 5.6 collective-permute-start.64
  645.5 5.6 collective-permute-start.66
  651.7 5.3 collective-permute-start.68
  658.2 7.2 %collective-permute-start.70 = (f32[1,8,32]{2,1,0:T(8,128)S(1)}, f32[1,8,32]{2,1,0:T(8,128)S(1)}, u32[]{:S(2)}, u32[]{:S(2)}) collective-permute-start(f32[1,8,32]{2,1,0:T(8,128)S(1)} %get-tuple-element.98), channel_id=1, source_target_pairs={{64,0},{128,64},{192,128},{256,192},{320,256},{384,320},{448,384},... | collective-permute-start | bytes 3080 | tf_op jit(solution)/shard_map/ppermute | solution.py:23
  666.1 5.8 collective-permute-start.72
  674.0 7.2 %collective-permute-start.74 = (f32[1,16,64]{2,1,0:T(8,128)S(1)}, f32[1,16,64]{2,1,0:T(8,128)S(1)}, u32[]{:S(2)}, u32[]{:S(2)}) collective-permute-start(f32[1,16,64]{2,1,0:T(8,128)S(1)} %get-tuple-element.82), channel_id=1, source_target_pairs={{64,0},{128,64},{192,128},{256,192},{320,256},{384,320},{448,384},... | collective-permute-start | bytes 12296 | tf_op jit(solution)/shard_map/ppermute | solution.py:23
  676.1 5.8 collective-permute-start.75
  682.0 5.8 collective-permute-start.76
  692.5 7.0 collective-permute-start.78
  694.4 5.9 collective-permute-start.79
  700.4 5.8 collective-permute-start.80
  701.7 5.3 collective-permute-start.81
  (39 other events, 1696.1 us)
where the time goes:
time: 724 us; the launch traced here: 709 us
  starting transfers between devices  286 us (40%)
  blocking collectives  285 us (39%)
  local copies, waits for them, and re-layouts  50.6 us (7%)
  other arithmetic  48.4 us (7%)
  between operations  23.8 us (3%)
  waiting for transfers between devices  16.1 us (2%)
    ppermute x41, starting transfers between devices, padded_2(): lax.ppermute(tail, axis, [(i, (i + 1) % count) for i in range(ends)])  165 us
    ppermute x41, starting transfers between devices, padded_2(): lax.ppermute(head, axis, [((i + 1) % count, i) for i in range(ends)])  121 us
    all_gather x1, blocking collectives, per_device(): lax.all_gather(weight, 'yz', axis=1, tiled=True)  83 us
    all_gather x1, blocking collectives, per_device(): lax.all_gather(residual, 'yz', axis=1, tiled=True)  62.1 us
    psum x4, blocking collectives, stabilized_solve(): rho_now = lax.psum(jnp.sum(source * residual), 'gx')  53.7 us
    psum x4, blocking collectives, stabilized_solve(): lax.psum((jnp.sum(bent_image * middle), jnp.sum(bent_image * bent_image))...  50.5 us
    reshape x4, local copies, waits for them, and re-layouts, restrict(): values.reshape(values.shape[0] // 2, 2, values.shape[1] // 2, 2, values.s...  40 us
    psum x3, blocking collectives, stabilized_solve(): step_alpha = rho_now / lax.psum(jnp.sum(source * applied), 'gx')  35.7 us
  transfers between devices with their start and end apart: 82, of which 20 were waited for; matrix products, arithmetic and copies ran while one was open for 6% of the time, Pallas kernels for 0%

commit v1 on v0

v1 whole, which is shorter than its diff:
```python
import jax
import jax.numpy as jnp
from jax import lax
from jax.experimental import pallas as pl
from jax.experimental.pallas import tpu as pltpu
from jax.sharding import PartitionSpec as P

MESH = pl.DeviceIdType.MESH
BITERS = 4
OMEGA = 0.8
NG = 8
NQ = 64
F32 = jnp.float32


def roll(v, by):
    return pltpu.roll(v, by % 128, 1)


def lanes_of(rows):
    return lax.broadcasted_iota(jnp.int32, (rows, 128), 1)


def swap(v, bit):
    lane = lanes_of(v.shape[0])
    return jnp.where((lane & bit) == 0, roll(v, -bit), roll(v, bit))


class Level:
    def __init__(self, scale, rows, start, count, unit, planes, depth, pieces):
        self.half = 0.5 * scale
        self.rows = rows
        self.start = start
        self.unit = unit
        self.planes = planes
        self.depth = depth

    def load(self, ref, i, shift=0):
        return ref[i, pl.ds(self.start + shift, self.rows), :]

    def store(self, ref, i, v):
        ref[i, pl.ds(self.start, self.rows), :] = v

    def shifted(self, ref, i):
        c = self.load(ref, i)
        if self.planes == 1:
            xp, xm = self.load(ref, i + 1), self.load(ref, i - 1)
        else:
            n, s = self.planes, self.unit
            field = (lanes_of(self.rows) // s) & (n - 1)
            xp = jnp.where(field < n - 1, roll(c, -s), roll(self.load(ref, i + 1), (n - 1) * s))
            xm = jnp.where(field > 0, roll(c, s), roll(self.load(ref, i - 1), -(n - 1) * s))
        yp, ym = self.load(ref, i, 1), self.load(ref, i, -1)
        zp, zm = roll(c, -self.depth), roll(c, self.depth)
        return c, (xp, xm, yp, ym, zp, zm)

    def weigh(self, i):
        lane = lanes_of(self.rows)
        first, last = lane < self.depth, lane >= 128 - self.depth
        c, others = self.shifted(self.b, i)
        total = None
        for k, other in enumerate(others):
            edge = {4: last, 5: first}.get(k)
            if edge is not None:
                other = jnp.where(edge, 0.0, other)
            w = self.half * (c + other)
            total = w if total is None else total + w
            if edge is not None:
                w = jnp.where(edge, 0.0, w)
            self.w[k, i, pl.ds(self.start, self.rows), :] = w
        self.store(self.d, i, total)
        inside = c > 0.0
        self.store(self.inv, i, jnp.where(inside, OMEGA / jnp.where(inside, total, 1.0), 0.0))

    def first(self, i):
        self.store(self.v, i, self.load(self.inv, i) * self.load(self.f, i))

    def around(self, ref, i):
        c, others = self.shifted(ref, i)
        total = None
        for k, other in enumerate(others):
            term = self.w[k, i, pl.ds(self.start, self.rows), :] * other
            total = term if total is None else total + term
        return c, total

    def smooth(self, src, i):
        c, s = self.around(src, i)
        return (1.0 - OMEGA) * c + self.load(self.inv, i) * (self.load(self.f, i) + s)

    def residual(self, i):
        c, s = self.around(self.u, i)
        return self.load(self.f, i) + s - self.load(self.d, i) * c


def each(lo, hi, body, group=None):
    if group is None:
        for i in range(lo, hi):
            body(i)
    else:
        assert (hi - lo) % group == 0

        def step(t, carry):
            for k in range(group):
                body(lo + t * group + k)
            return carry

        lax.fori_loop(0, (hi - lo) // group, step, 0)


R0, O0 = 56, 12
R1, O1 = 40, 12
R2, O2 = 40, 16
R3, O3 = 32, 16

LEVEL_SHAPES = ((22, R0), (10, R1), (10, R2), (10, R3))


def kernel(f_hbm, b_hbm, out, *refs):
    refs = list(refs)

    def take(n):
        got = refs[:n]
        del refs[:n]
        return got

    lv = [
        Level(1.0, 40, 8, 16, 1, 1, 1, 1),
        Level(0.25, 24, 8, 4, 1, 2, 2, 1),
        Level(0.0625, 24, 8, 8, 1, 4, 4, 1),
        Level(0.015625, 16, 8, 8, 2, 2, 8, 1),
    ]
    for one in lv:
        one.b, one.f, one.v, one.u, one.d, one.inv, one.w = take(7)
    pair, b2_own, f2_own, gathered, e_pad = take(5)
    load_sem, send_sem, near_recv, wide_recv, far_recv = take(5)
    l0, l1, l2, l3 = lv

    g, q = lax.axis_index("gx"), lax.axis_index("yz")

    load_b = pltpu.make_async_copy(b_hbm, l0.b.at[pl.ds(3, 16), pl.ds(O0, 32)], load_sem.at[0])
    load_f = pltpu.make_async_copy(f_hbm, l0.f.at[pl.ds(3, 16), pl.ds(O0, 32)], load_sem.at[1])
    load_b.start()
    load_f.start()

    def device(dg, dq):
        return {"gx": lax.rem(g + dg + NG, NG), "yz": lax.rem(q + dq + NQ, NQ)}

    near = [(dg, dq) for dg in (-1, 0, 1) for dq in (-1, 0, 1) if dg or dq]
    wide = [(dg, dq) for dg in (4, 3, 5, 2, 6, 1, 7, 0) for dq in (-1, 1, 0) if dg or dq]

    def yz_order():
        order = []
        for d in range(1, NQ):
            z, x = d % 16, d // 16
            order.append((-(min(z, 16 - z) + min(x, 4 - x)), d))
        return [d for _, d in sorted(order)]

    far = yz_order()

    barrier = pltpu.get_barrier_semaphore()

    def greet(target):
        pl.semaphore_signal(barrier, inc=1, device_id=target, device_id_type=MESH)

    for d in far:
        if d not in (1, NQ - 1):
            greet(device(0, d))
    for dg, dq in wide:
        greet(device(dg, dq))

    for one, (blocks, rows) in ((l1, LEVEL_SHAPES[1]), (l2, LEVEL_SHAPES[2]), (l3, LEVEL_SHAPES[3])):
        for ref in (one.b, one.v, one.u):
            for i in (0, blocks - 1):
                ref[i] = jnp.zeros((rows, 128), F32)
    for ref in (l3.b, l3.f):
        for i in range(1, 9):
            ref[i] = jnp.zeros((R3, 128), F32)
    e_pad[pl.ds(0, 8), :] = jnp.zeros((8, 128), F32)
    e_pad[pl.ds(72, 8), :] = jnp.zeros((8, 128), F32)

    even = (lanes_of(16) & 1) == 0

    def restrict_0(make, store):
        def body(i):
            halves = []
            for half in range(2):
                slot = 2 * i + half
                pair[slot, pl.ds(0, 32), :] = make(2 * slot) + make(2 * slot + 1)
                t = pair[slot, pl.ds(0, 16, stride=2), :] + pair[slot, pl.ds(1, 16, stride=2), :]
                halves.append(t + swap(t, 1))
            store(i, 0.125 * jnp.where(even, halves[0], halves[1]))

        return body

    def restrict_1(make, rows):
        lane = lanes_of(rows)
        packed = None
        for i in range(4):
            pair[i, pl.ds(0, 2 * rows), :] = make(i)
            t = pair[i, pl.ds(0, rows, stride=2), :] + pair[i, pl.ds(1, rows, stride=2), :]
            t = t + swap(t, 1)
            t = t + swap(t, 2)
            packed = t if packed is None else jnp.where((lane & 3) == i, t, packed)
        return 0.125 * packed

    def restrict_2(make):
        def one(i):
            pair[i, pl.ds(0, 24), :] = make(i)
            t = pair[i, pl.ds(0, 12, stride=2), :] + pair[i, pl.ds(1, 12, stride=2), :]
            t = t + swap(t, 1)
            return 0.125 * (t + swap(t, 4))

        return one

    def restrict_3(make):
        k = lanes_of(1) & 15
        row = None
        for i in range(8):
            pair[i, pl.ds(0, 4), :] = make(i)
            t = pair[i, pl.ds(0, 2, stride=2), :] + pair[i, pl.ds(1, 2, stride=2), :]
            t = t + swap(t, 2)
            t = 0.125 * (t + swap(t, 8))
            for j in range(2):
                row = t[j : j + 1] if row is None else jnp.where(k == 2 * i + j, t[j : j + 1], row)
        return row

    load_b.wait()

    def store_b1(i, v):
        l1.b[3 + i, pl.ds(O1, 16), :] = v

    each(0, 4, restrict_0(lambda p: l0.b[3 + p, pl.ds(O0, 32), :], store_b1))
    load_f.wait()

    pl.semaphore_wait(barrier, 61 + 23)

    pending = []

    def cut(d, first, size, width):
        if d == 0:
            return first, first, size
        if d > 0:
            return first + size - width, first - width, width
        return first, first + size, width

    def send_near(slot, ref, blocks, rows, block_width, row_width):
        copies = []
        for n, (dg, dq) in enumerate(near):
            bs, bt, bn = cut(dg, blocks[0], blocks[1], block_width)
            rs, rt, rn = cut(dq, rows[0], rows[1], row_width)
            copy = pltpu.make_async_remote_copy(
                src_ref=ref.at[pl.ds(bs, bn), pl.ds(rs, rn)],
                dst_ref=ref.at[pl.ds(bt, bn), pl.ds(rt, rn)],
                send_sem=send_sem.at[slot, n],
                recv_sem=near_recv.at[slot, n],
                device_id=device(dg, dq),
                device_id_type=MESH,
            )
            copy.start()
            copies.append(copy)
        pending.extend(copies)
        return copies

    def arrive(copies):
        for copy in copies:
            copy.wait_recv()

    b0_copies = send_near(0, l0.b, (3, 16), (O0, 32), 3, 3)
    f0_copies = send_near(1, l0.f, (3, 16), (O0, 32), 2, 2)
    b1_copies = send_near(2, l1.b, (3, 4), (O1, 16), 2, 4)

    def clear(ref, blocks, rows, total_blocks, block_width, row_width):
        first, count = blocks
        start, height = rows

        @pl.when(g == 0)
        def _():
            for i in range(first - block_width, first):
                ref[i] = jnp.zeros(ref.shape[1:], F32)

        @pl.when(g == NG - 1)
        def _():
            for i in range(first + count, first + count + block_width):
                ref[i] = jnp.zeros(ref.shape[1:], F32)

        @pl.when(q == 0)
        def _():
            for i in range(first - block_width, first + count + block_width):
                ref[i, pl.ds(start - row_width, row_width), :] = jnp.zeros((row_width, 128), F32)

        @pl.when(q == NQ - 1)
        def _():
            for i in range(first - block_width, first + count + block_width):
                ref[i, pl.ds(start + height, row_width), :] = jnp.zeros((row_width, 128), F32)

    arrive(b0_copies)
    clear(l0.b, (3, 16), (O0, 32), 22, 3, 3)
    each(1, 21, l0.weigh, 2)
    arrive(f0_copies)
    each(1, 21, l0.first, 4)
    each(2, 20, lambda i: l0.store(l0.u, i, l0.smooth(l0.v, i)), 2)

    def store_f1(i, v):
        l1.f[3 + i, pl.ds(O1, 16), :] = v

    each(0, 4, restrict_0(lambda p: l0.residual(3 + p)[O0 - 8 : O0 - 8 + 32], store_f1))
    f1_copies = send_near(3, l1.f, (3, 4), (O1, 16), 2, 4)

    arrive(b1_copies)
    clear(l1.b, (3, 4), (O1, 16), 10, 2, 4)
    b2_own[pl.ds(7, 10), :] = restrict_1(lambda i: l1.b[3 + i, pl.ds(O1 - 2, 20), :], 10)

    def send_wide(slot, parts):
        copies = []
        for n, (dg, dq) in enumerate(wide):
            src, dst = parts(dq)
            copy = pltpu.make_async_remote_copy(
                src_ref=src,
                dst_ref=dst,
                send_sem=send_sem.at[4 + slot, n],
                recv_sem=wide_recv.at[slot, n],
                device_id=device(dg, dq),
                device_id_type=MESH,
            )
            copy.start()
            copies.append(copy)
        pending.extend(copies)
        return copies

    def b2_parts(dq):
        src, dst, n = {0: (8, O2, 8), 1: (7, O2 - 9, 9), -1: (8, O2 + 8, 9)}[dq]
        return b2_own.at[pl.ds(src, n)], l2.b.at[1 + g, pl.ds(dst, n)]

    b2_copies = send_wide(0, b2_parts)
    l2.b[1 + g, pl.ds(O2, 8), :] = b2_own[pl.ds(8, 8), :]
    each(1, 9, l1.weigh)
    arrive(f1_copies)
    each(1, 9, l1.first)
    each(2, 8, lambda i: l1.store(l1.u, i, l1.smooth(l1.v, i)))
    f2_own[...] = restrict_1(lambda i: l1.residual(3 + i)[O1 - 8 : O1 - 8 + 16], 8)

    def f2_parts(dq):
        return f2_own, l2.f.at[1 + g, pl.ds(O2 - 8 * dq, 8)]

    f2_copies = send_wide(1, f2_parts)
    l2.f[1 + g, pl.ds(O2, 8), :] = f2_own[...]

    arrive(b2_copies)

    @pl.when(q == 0)
    def _():
        for i in range(1, 9):
            l2.b[i, pl.ds(O2 - 9, 9), :] = jnp.zeros((9, 128), F32)

    @pl.when(q == NQ - 1)
    def _():
        for i in range(1, 9):
            l2.b[i, pl.ds(O2 + 8, 9), :] = jnp.zeros((9, 128), F32)

    each(1, 9, l2.weigh)
    b3_of = restrict_2(lambda i: l2.load(l2.b, i))

    def store_b3(i):
        l3.b[i, pl.ds(O3 - 4, 12), :] = b3_of(i)

    each(1, 9, store_b3)
    each(1, 9, l3.weigh)
    b4 = restrict_3(lambda i: l3.b[1 + i, pl.ds(O3, 4), :])

    arrive(f2_copies)
    each(1, 9, l2.first)
    each(1, 9, lambda i: l2.store(l2.u, i, l2.smooth(l2.v, i)))
    f3_of = restrict_2(l2.residual)

    def store_f3(i):
        l3.f[i, pl.ds(O3 - 4, 12), :] = f3_of(i)

    each(1, 9, store_f3)
    each(1, 9, l3.first)
    each(1, 9, lambda i: l3.store(l3.u, i, l3.smooth(l3.v, i)))
    f4 = restrict_3(lambda i: l3.residual(1 + i)[O3 - 8 : O3 - 8 + 4])

    gathered[pl.ds(2 * q, 1), :] = f4
    gathered[pl.ds(2 * q + 1, 1), :] = b4
    far_copies = []
    for n, d in enumerate(far):
        here = gathered.at[pl.ds(2 * q, 2)]
        copy = pltpu.make_async_remote_copy(
            src_ref=here,
            dst_ref=here,
            send_sem=send_sem.at[6, n],
            recv_sem=far_recv.at[n],
            device_id=device(0, d),
            device_id_type=MESH,
        )
        copy.start()
        far_copies.append(copy)
    pending.extend(far_copies)
    arrive(far_copies)

    source = gathered[pl.ds(0, NQ, stride=2), :]
    weight = gathered[pl.ds(1, NQ, stride=2), :]
    lane = lanes_of(NQ)
    row = lax.broadcasted_iota(jnp.int32, (NQ, 128), 0)
    odd = (lane & 1) == 1
    plane = (lane // 2) & 7
    edges = (
        plane == 7,
        plane == 0,
        (row == NQ - 1) & odd,
        (row == 0) & jnp.logical_not(odd),
        lane >= 112,
        lane < 16,
    )

    def bottom_shifts(v):
        up, down = roll(v, -1), roll(v, 1)
        yp = jnp.where(odd, pltpu.roll(down, NQ - 1, 0), up)
        ym = jnp.where(odd, down, pltpu.roll(up, 1, 0))
        return roll(v, -2), roll(v, 2), yp, ym, roll(v, -16), roll(v, 16)

    half = 0.5 * 0.25**4
    bottom_w = []
    bottom_d = None
    for edge, other in zip(edges, bottom_shifts(weight)):
        w = half * (weight + jnp.where(edge, 0.0, other))
        bottom_d = w if bottom_d is None else bottom_d + w
        bottom_w.append(jnp.where(edge, 0.0, w))

    def apply_op(v):
        result = bottom_d * v
        for w, other in zip(bottom_w, bottom_shifts(v)):
            result = result - w * other
        return result

    def total(v):
        return jnp.sum(v, keepdims=True)

    answer = None
    residual = source
    direction = source
    applied = None
    rho = total(source * source)
    rho_prev = rho
    alpha = omega = None
    for turn in range(BITERS):
        if turn > 0:
            beta = (rho / rho_prev) * (alpha / omega)
            direction = residual + beta * (direction - omega * applied)
        applied = apply_op(direction)
        alpha = rho / total(source * applied)
        middle = residual - alpha * applied
        bent = apply_op(middle)
        omega = total(bent * middle) / total(bent * bent)
        step = alpha * direction + omega * middle
        answer = step if answer is None else answer + step
        residual = middle - omega * bent
        if turn + 1 < BITERS:
            rho_prev = rho
            rho = total(source * residual)

    e_pad[pl.ds(8, NQ), :] = answer
    fine = lax.broadcasted_iota(jnp.int32, (16, 128), 0) - 8
    near_rows = jnp.where(
        fine < 0,
        e_pad[pl.ds(7 + q, 1), :],
        jnp.where(fine < 4, e_pad[pl.ds(8 + q, 1), :], e_pad[pl.ds(9 + q, 1), :]),
    )
    parity = jnp.where((fine < 0) | ((fine >= 2) & (fine < 4)), 1, 0)
    group = lanes_of(16) & ~15

    def pick(v, index):
        return jnp.take_along_axis(v, index, axis=1)

    def up_3(i):
        wide_e = pick(near_rows, group + parity + 2 * (i - 1))
        l3.store(l3.v, i, l3.load(l3.u, i) + wide_e)

    each(1, 9, up_3)

    def up_3s(i):
        v = l3.smooth(l3.v, i)
        v = v[6:14]
        for k in range(2):
            pair[i, pl.ds(k, 8, stride=2), :] = v
        mid = l2.u[i, pl.ds(O2 - 4, 16), :] + pair[i, pl.ds(0, 16), :]
        l2.v[i, pl.ds(O2 - 4, 16), :] = mid

    each(1, 9, up_3s)
    each(1, 9, lambda i: l2.store(l2.u, i, l2.smooth(l2.v, i)))

    spread = lanes_of(12) & ~3
    for i in range(-1, 5):
        from_block = 1 + g + (i // 4)
        v = pick(l2.u[from_block, pl.ds(O2 - 2, 12), :], spread + (i % 4))
        for k in range(2):
            pair[i + 1, pl.ds(k, 12, stride=2), :] = v
        l1.v[3 + i, pl.ds(O1 - 4, 24), :] = l1.u[3 + i, pl.ds(O1 - 4, 24), :] + pair[i + 1, pl.ds(0, 24), :]
    for i in range(-1, 5):
        l1.store(l1.u, 3 + i, l1.smooth(l1.v, 3 + i))

    even20 = (lanes_of(20) & 1) == 0
    for i in range(-1, 9):
        v = l1.u[3 + (i // 2), pl.ds(O1 - 2, 20), :]
        v = jnp.where(even20, v, roll(v, 1)) if i % 2 == 0 else jnp.where(even20, roll(v, -1), v)
        for k in range(2):
            pair[i + 1, pl.ds(k, 20, stride=2), :] = v
        wide_v = pair[i + 1, pl.ds(0, 40), :]
        for p in (2 * i, 2 * i + 1):
            if -1 <= p <= 16:
                l0.store(l0.v, 3 + p, l0.load(l0.u, 3 + p) + wide_v)

    def finish(p):
        out[p] = l0.smooth(l0.v, 3 + p)[O0 - 8 : O0 - 8 + 32]

    each(0, 16, finish, 2)

    for copy in pending:
        copy.wait_send()


def per_device(right_side, coefficient):
    scratch = []
    for blocks, rows in LEVEL_SHAPES:
        scratch += [pltpu.VMEM((blocks, rows, 128), F32)] * 6
        scratch.append(pltpu.VMEM((6, blocks, rows, 128), F32))
    scratch += [
        pltpu.VMEM((16, 48, 128), F32),
        pltpu.VMEM((24, 128), F32),
        pltpu.VMEM((8, 128), F32),
        pltpu.VMEM((2 * NQ, 128), F32),
        pltpu.VMEM((80, 128), F32),
        pltpu.SemaphoreType.DMA((2,)),
        pltpu.SemaphoreType.DMA((7, 64)),
        pltpu.SemaphoreType.DMA((4, 8)),
        pltpu.SemaphoreType.DMA((2, 23)),
        pltpu.SemaphoreType.DMA((63,)),
    ]
    return pl.pallas_call(
        kernel,
        out_shape=jax.ShapeDtypeStruct((16, 32, 128), F32),
        in_specs=[pl.BlockSpec(memory_space=pl.ANY)] * 2,
        out_specs=pl.BlockSpec(memory_space=pltpu.VMEM),
        scratch_shapes=scratch,
        compiler_params=pltpu.CompilerParams(
            collective_id=0, has_side_effects=True, vmem_limit_bytes=40 * 2**20
        ),
        cost_estimate=pl.CostEstimate(flops=10_000_000, bytes_accessed=3 * 262144, transcendentals=0),
    )(right_side, coefficient)


def solution(mesh):
    return jax.shard_map(
        per_device,
        mesh=mesh,
        in_specs=(P("gx", "yz", None), P("gx", "yz", None)),
        out_specs=P("gx", "yz", None),
        check_vma=False,
    )
```

time: 724 us -> 54.2 us (0.07); the launches traced: 709 us -> 54 us
  starting transfers between devices: 286 us -> 0 us
  blocking collectives: 285 us -> 0 us
  Pallas kernels: 0 us -> 51.4 us
  other arithmetic: 48.4 us -> 0 us
  local copies, waits for them, and re-layouts: 50.6 us -> 2.6 us
  between operations: 23.8 us -> 0.01 us
  waiting for transfers between devices: 16.1 us -> 0 us
    ppermute x82 -> x0, starting transfers between devices: 286 us -> none  [the longest x41 165 us: padded_2(): lax.ppermute(tail, axis, [(i, (i + 1) % count) for i in range(ends)])]
    all_gather x2 -> x0, blocking collectives: 145 us -> none  [the longest x1 83 us: per_device(): lax.all_gather(weight, 'yz', axis=1, tiled=True)]
    psum x11 -> x0, blocking collectives: 140 us -> none  [the longest x4 53.7 us: stabilized_solve(): rho_now = lax.psum(jnp.sum(source * residual), 'gx')]
    pallas_call x0 -> x1, Pallas kernels: none -> 51.4 us  [per_device(): pl.pallas_call(kernel, out_shape=jax.ShapeDtypeStruct((16, 32, 128), F32)...]
    reshape x10 -> x0, local copies, waits for them, and re-layouts: 41.9 us -> none  [the longest x4 40 us: restrict(): values.reshape(values.shape[0] // 2, 2, values.shape[1] // 2, 2, values.s...]
    reduce_sum x22 -> x0, other arithmetic: 25.9 us -> none  [the longest x10 17.5 us: restrict(): return values.reshape(values.shape[0] // 2, 2, values.shape[1] // 2, 2, v...]
    ppermute x82 -> x0, waiting for transfers between devices: 16.1 us -> none  [the longest x41 15.9 us: padded_2(): lax.ppermute(tail, axis, [(i, (i + 1) % count) for i in range(ends)])]
    add x16 -> x0, other arithmetic: 8.08 us -> none  [the longest x8 7.95 us: per_device(): iterate + RELAXATION * (source - operate(padder(iterate), face_list, leve...]
  transfers between devices with their start and end apart: 82 -> 0, of which waited for: 20 -> 0; matrix products, arithmetic and copies ran while one was open for 6% -> 0% of each run, Pallas kernels for 0% -> 0%
where the time goes in v1:
time: 54.2 us; the launch traced here: 54 us
  Pallas kernels  51.4 us (95%)
  local copies, waits for them, and re-layouts  2.6 us (5%)
    pallas_call x1, Pallas kernels, per_device(): pl.pallas_call(kernel, out_shape=jax.ShapeDtypeStruct((16, 32, 128), F32)...  51.4 us
    unnamed x5, local copies, waits for them, and re-layouts  2.6 us

profile of v1, /device:TPU:1, one launch (start us, length us, event | category | flops | bytes accessed | tf_op | source)
XLA Modules:
  0.0 54.0 jit_solution(2489708472519334600)
XLA Ops:
  0.0 0.0 copy-start
  0.0 0.9 %copy-done = f32[16,32,128]{2,1,0:T(8,128)S(1)} copy-done((f32[16,32,128]{2,1,0:T(8,128)S(1)}, f32[16,32,128]{2,1,0:T(8,128)}, u32[]{:S(2)}) %copy-start) | copy-done | bytes 262168
  1.0 0.0 copy-start.1
  1.0 0.9 %copy-done.1 = f32[16,32,128]{2,1,0:T(8,128)S(1)} copy-done((f32[16,32,128]{2,1,0:T(8,128)S(1)}, f32[16,32,128]{2,1,0:T(8,128)}, u32[]{:S(2)}) %copy-start.1) | copy-done | bytes 262168
  1.9 51.4 %shard_map.28 = f32[16,32,128]{2,1,0:T(8,128)S(1)} custom-call(f32[16,32,128]{2,1,0:T(8,128)S(1)} %copy-done, f32[16,32,128]{2,1,0:T(8,128)S(1)} %copy-done.1), custom_call_target="tpu_custom_call" | custom-call | flops 10000000 | bytes 786432 | tf_op jit(solution)/shard_map/pallas_call | solution.py:539
  53.3 0.7 %copy.4 = f32[16,32,128]{2,1,0:T(8,128)} copy(f32[16,32,128]{2,1,0:T(8,128)S(1)} %shard_map.28) | data formatting | bytes 524288
Async XLA Ops:
  0.0 0.9 %copy-start = (f32[16,32,128]{2,1,0:T(8,128)S(1)}, f32[16,32,128]{2,1,0:T(8,128)}, u32[]{:S(2)}) copy-start(f32[16,32,128]{2,1,0:T(8,128)} %f_hbm.1) | copy-start | bytes 786436
  1.0 0.9 %copy-start.1 = (f32[16,32,128]{2,1,0:T(8,128)S(1)}, f32[16,32,128]{2,1,0:T(8,128)}, u32[]{:S(2)}) copy-start(f32[16,32,128]{2,1,0:T(8,128)} %b_hbm.1) | copy-start | bytes 786436

commit v2 on v1

--- a/solution.py
+++ b/solution.py
@@ -114,6 +114,8 @@
 
 LEVEL_SHAPES = ((22, R0), (10, R1), (10, R2), (10, R3))
 
+GROUP_ROWS = ((6, 54), (13, 16), (16, 8), (16, 8), (5, 40), (4, 46), (3, 42))
+
 
 def kernel(f_hbm, b_hbm, out, *refs):
     refs = list(refs)
@@ -132,7 +134,7 @@
     for one in lv:
         one.b, one.f, one.v, one.u, one.d, one.inv, one.w = take(7)
     pair, b2_own, f2_own, gathered, e_pad = take(5)
-    load_sem, send_sem, near_recv, wide_recv, far_recv = take(5)
+    load_sem, send_sem, recv_sem = take(3)
     l0, l1, l2, l3 = lv
 
     g, q = lax.axis_index("gx"), lax.axis_index("yz")
@@ -234,8 +236,6 @@
 
     pl.semaphore_wait(barrier, 61 + 23)
 
-    pending = []
-
     def cut(d, first, size, width):
         if d == 0:
             return first, first, size
@@ -244,30 +244,29 @@
         return first, first + size, width
 
     def send_near(slot, ref, blocks, rows, block_width, row_width):
-        copies = []
-        for n, (dg, dq) in enumerate(near):
+        for dg, dq in near:
             bs, bt, bn = cut(dg, blocks[0], blocks[1], block_width)
             rs, rt, rn = cut(dq, rows[0], rows[1], row_width)
             copy = pltpu.make_async_remote_copy(
                 src_ref=ref.at[pl.ds(bs, bn), pl.ds(rs, rn)],
                 dst_ref=ref.at[pl.ds(bt, bn), pl.ds(rt, rn)],
-                send_sem=send_sem.at[slot, n],
-                recv_sem=near_recv.at[slot, n],
+                send_sem=send_sem.at[slot],
+                recv_sem=recv_sem.at[slot],
                 device_id=device(dg, dq),
                 device_id_type=MESH,
             )
             copy.start()
-            copies.append(copy)
-        pending.extend(copies)
-        return copies
-
-    def arrive(copies):
-        for copy in copies:
-            copy.wait_recv()
-
-    b0_copies = send_near(0, l0.b, (3, 16), (O0, 32), 3, 3)
-    f0_copies = send_near(1, l0.f, (3, 16), (O0, 32), 2, 2)
-    b1_copies = send_near(2, l1.b, (3, 4), (O1, 16), 2, 4)
+
+    def all_of(sem, shape):
+        some = l0.w.at[(0,) + tuple(pl.ds(0, n) for n in shape)]
+        return pltpu.make_async_copy(some, some, sem)
+
+    def arrive(group):
+        all_of(recv_sem.at[group], GROUP_ROWS[group]).wait()
+
+    send_near(0, l0.b, (3, 16), (O0, 32), 3, 3)
+    send_near(1, l0.f, (3, 16), (O0, 32), 2, 2)
+    send_near(2, l1.b, (3, 4), (O1, 16), 2, 4)
 
     def clear(ref, blocks, rows, total_blocks, block_width, row_width):
         first, count = blocks
@@ -293,48 +292,44 @@
             for i in range(first - block_width, first + count + block_width):
                 ref[i, pl.ds(start + height, row_width), :] = jnp.zeros((row_width, 128), F32)
 
-    arrive(b0_copies)
+    arrive(0)
     clear(l0.b, (3, 16), (O0, 32), 22, 3, 3)
-    each(1, 21, l0.weigh, 2)
-    arrive(f0_copies)
-    each(1, 21, l0.first, 4)
-    each(2, 20, lambda i: l0.store(l0.u, i, l0.smooth(l0.v, i)), 2)
+    each(1, 21, l0.weigh, 10)
+    arrive(1)
+    each(1, 21, l0.first, 10)
+    each(2, 20, lambda i: l0.store(l0.u, i, l0.smooth(l0.v, i)), 9)
 
     def store_f1(i, v):
         l1.f[3 + i, pl.ds(O1, 16), :] = v
 
     each(0, 4, restrict_0(lambda p: l0.residual(3 + p)[O0 - 8 : O0 - 8 + 32], store_f1))
-    f1_copies = send_near(3, l1.f, (3, 4), (O1, 16), 2, 4)
-
-    arrive(b1_copies)
+    send_near(3, l1.f, (3, 4), (O1, 16), 2, 4)
+
+    arrive(2)
     clear(l1.b, (3, 4), (O1, 16), 10, 2, 4)
     b2_own[pl.ds(7, 10), :] = restrict_1(lambda i: l1.b[3 + i, pl.ds(O1 - 2, 20), :], 10)
 
     def send_wide(slot, parts):
-        copies = []
-        for n, (dg, dq) in enumerate(wide):
+        for dg, dq in wide:
             src, dst = parts(dq)
             copy = pltpu.make_async_remote_copy(
                 src_ref=src,
                 dst_ref=dst,
-                send_sem=send_sem.at[4 + slot, n],
-                recv_sem=wide_recv.at[slot, n],
+                send_sem=send_sem.at[slot],
+                recv_sem=recv_sem.at[slot],
                 device_id=device(dg, dq),
                 device_id_type=MESH,
             )
             copy.start()
-            copies.append(copy)
-        pending.extend(copies)
-        return copies
 
     def b2_parts(dq):
         src, dst, n = {0: (8, O2, 8), 1: (7, O2 - 9, 9), -1: (8, O2 + 8, 9)}[dq]
         return b2_own.at[pl.ds(src, n)], l2.b.at[1 + g, pl.ds(dst, n)]
 
-    b2_copies = send_wide(0, b2_parts)
+    send_wide(4, b2_parts)
     l2.b[1 + g, pl.ds(O2, 8), :] = b2_own[pl.ds(8, 8), :]
     each(1, 9, l1.weigh)
-    arrive(f1_copies)
+    arrive(3)
     each(1, 9, l1.first)
     each(2, 8, lambda i: l1.store(l1.u, i, l1.smooth(l1.v, i)))
     f2_own[...] = restrict_1(lambda i: l1.residual(3 + i)[O1 - 8 : O1 - 8 + 16], 8)
@@ -342,10 +337,10 @@
     def f2_parts(dq):
         return f2_own, l2.f.at[1 + g, pl.ds(O2 - 8 * dq, 8)]
 
-    f2_copies = send_wide(1, f2_parts)
+    send_wide(5, f2_parts)
     l2.f[1 + g, pl.ds(O2, 8), :] = f2_own[...]
 
-    arrive(b2_copies)
+    arrive(4)
 
     @pl.when(q == 0)
     def _():
@@ -367,7 +362,7 @@
     each(1, 9, l3.weigh)
     b4 = restrict_3(lambda i: l3.b[1 + i, pl.ds(O3, 4), :])
 
-    arrive(f2_copies)
+    arrive(5)
     each(1, 9, l2.first)
     each(1, 9, lambda i: l2.store(l2.u, i, l2.smooth(l2.v, i)))
     f3_of = restrict_2(l2.residual)
@@ -382,21 +377,18 @@
 
     gathered[pl.ds(2 * q, 1), :] = f4
     gathered[pl.ds(2 * q + 1, 1), :] = b4
-    far_copies = []
-    for n, d in enumerate(far):
+    for d in far:
         here = gathered.at[pl.ds(2 * q, 2)]
         copy = pltpu.make_async_remote_copy(
             src_ref=here,
             dst_ref=here,
-            send_sem=send_sem.at[6, n],
-            recv_sem=far_recv.at[n],
+            send_sem=send_sem.at[6],
+            recv_sem=recv_sem.at[6],
             device_id=device(0, d),
             device_id_type=MESH,
         )
         copy.start()
-        far_copies.append(copy)
-    pending.extend(far_copies)
-    arrive(far_copies)
+    arrive(6)
 
     source = gathered[pl.ds(0, NQ, stride=2), :]
     weight = gathered[pl.ds(1, NQ, stride=2), :]
@@ -513,10 +505,10 @@
     def finish(p):
         out[p] = l0.smooth(l0.v, 3 + p)[O0 - 8 : O0 - 8 + 32]
 
-    each(0, 16, finish, 2)
-
-    for copy in pending:
-        copy.wait_send()
+    each(0, 16, finish, 8)
+
+    for group, shape in enumerate(GROUP_ROWS):
+        all_of(send_sem.at[group], shape).wait()
 
 
 def per_device(right_side, coefficient):
@@ -531,19 +523,17 @@
         pltpu.VMEM((2 * NQ, 128), F32),
         pltpu.VMEM((80, 128), F32),
         pltpu.SemaphoreType.DMA((2,)),
-        pltpu.SemaphoreType.DMA((7, 64)),
-        pltpu.SemaphoreType.DMA((4, 8)),
-        pltpu.SemaphoreType.DMA((2, 23)),
-        pltpu.SemaphoreType.DMA((63,)),
+        pltpu.SemaphoreType.DMA((7,)),
+        pltpu.SemaphoreType.DMA((7,)),
     ]
     return pl.pallas_call(
         kernel,
         out_shape=jax.ShapeDtypeStruct((16, 32, 128), F32),
-        in_specs=[pl.BlockSpec(memory_space=pl.ANY)] * 2,
+        in_specs=[pl.BlockSpec(memory_space=pltpu.HBM)] * 2,
         out_specs=pl.BlockSpec(memory_space=pltpu.VMEM),
         scratch_shapes=scratch,
         compiler_params=pltpu.CompilerParams(
-            collective_id=0, has_side_effects=True, vmem_limit_bytes=40 * 2**20
+            collective_id=0, has_side_effects=True, vmem_limit_bytes=60 * 2**20
         ),
         cost_estimate=pl.CostEstimate(flops=10_000_000, bytes_accessed=3 * 262144, transcendentals=0),
     )(right_side, coefficient)

time: 54.2 us -> 47 us (0.87)
  Pallas kernels: 51.4 us -> 45.2 us
  local copies, waits for them, and re-layouts: 2.6 us -> 1.67 us
    pallas_call x1, Pallas kernels: 51.4 us -> 45.2 us  [per_device(): pl.pallas_call(kernel, out_shape=jax.ShapeDtypeStruct((16, 32, 128), F32)...]
    unnamed x5 -> x1, local copies, waits for them, and re-layouts: 2.6 us -> 1.67 us
where the time goes in v2:
time: 47 us; the launch traced here: 46.9 us
  Pallas kernels  45.2 us (96%)
  local copies, waits for them, and re-layouts  1.67 us (4%)
    pallas_call x1, Pallas kernels, per_device(): pl.pallas_call(kernel, out_shape=jax.ShapeDtypeStruct((16, 32, 128), F32)...  45.2 us
    unnamed x1, local copies, waits for them, and re-layouts  1.67 us

profile of v2, /device:TPU:1, one launch (start us, length us, event | category | flops | bytes accessed | tf_op | source)
XLA Modules:
  0.0 46.9 jit_solution(11043543321062315798)
XLA Ops:
  0.0 45.2 %shard_map.28 = f32[16,32,128]{2,1,0:T(8,128)} custom-call(f32[16,32,128]{2,1,0:T(8,128)} %f_hbm.1, f32[16,32,128]{2,1,0:T(8,128)} %b_hbm.1), custom_call_target="tpu_custom_call" | custom-call | flops 10000000 | bytes 786432 | tf_op jit(solution)/shard_map/pallas_call | solution.py:529
  45.2 1.7 %copy.4 = f32[16,32,128]{2,1,0:T(8,128)} copy(f32[16,32,128]{2,1,0:T(8,128)} %shard_map.28) | data formatting | bytes 524288

commit v3 on v2

--- a/solution.py
+++ b/solution.py
@@ -46,10 +46,11 @@
         if self.planes == 1:
             xp, xm = self.load(ref, i + 1), self.load(ref, i - 1)
         else:
-            n, s = self.planes, self.unit
-            field = (lanes_of(self.rows) // s) & (n - 1)
-            xp = jnp.where(field < n - 1, roll(c, -s), roll(self.load(ref, i + 1), (n - 1) * s))
-            xm = jnp.where(field > 0, roll(c, s), roll(self.load(ref, i - 1), -(n - 1) * s))
+            s = self.unit
+            bits = (self.planes - 1) * s
+            field = lanes_of(self.rows) & bits
+            xp = jnp.where(field != bits, roll(c, -s), roll(self.load(ref, i + 1), bits))
+            xm = jnp.where(field != 0, roll(c, s), roll(self.load(ref, i - 1), -bits))
         yp, ym = self.load(ref, i, 1), self.load(ref, i, -1)
         zp, zm = roll(c, -self.depth), roll(c, self.depth)
         return c, (xp, xm, yp, ym, zp, zm)
@@ -134,7 +135,7 @@
     for one in lv:
         one.b, one.f, one.v, one.u, one.d, one.inv, one.w = take(7)
     pair, b2_own, f2_own, gathered, e_pad = take(5)
-    load_sem, send_sem, recv_sem = take(3)
+    load_sem, send_sem, recv_sem, ready = take(4)
     l0, l1, l2, l3 = lv
 
     g, q = lax.axis_index("gx"), lax.axis_index("yz")
@@ -147,7 +148,7 @@
     def device(dg, dq):
         return {"gx": lax.rem(g + dg + NG, NG), "yz": lax.rem(q + dq + NQ, NQ)}
 
-    near = [(dg, dq) for dg in (-1, 0, 1) for dq in (-1, 0, 1) if dg or dq]
+    near = [(dg, dq) for dg in (-1, 1) for dq in (-1, 1)] + [(0, -1), (0, 1), (-1, 0), (1, 0)]
     wide = [(dg, dq) for dg in (4, 3, 5, 2, 6, 1, 7, 0) for dq in (-1, 1, 0) if dg or dq]
 
     def yz_order():
@@ -164,11 +165,15 @@
     def greet(target):
         pl.semaphore_signal(barrier, inc=1, device_id=target, device_id_type=MESH)
 
-    for d in far:
-        if d not in (1, NQ - 1):
-            greet(device(0, d))
-    for dg, dq in wide:
-        greet(device(dg, dq))
+    def device_xz(dx, dz):
+        return {"gx": g, "yz": ((q >> 4) + dx & 3) * 16 + (q + dz & 15)}
+
+    greeted = [device(dg, dq) for dg, dq in near]
+    greeted += [device(dg, dq) for dg in (-2, 2) for dq in (-1, 0, 1)]
+    greeted += [device_xz(0, dz) for dz in (1, -1, 2, -2, 3, -3)]
+    greeted += [device_xz(dx, 0) for dx in (1, 2, 3)]
+    for target in greeted:
+        greet(target)
 
     for one, (blocks, rows) in ((l1, LEVEL_SHAPES[1]), (l2, LEVEL_SHAPES[2]), (l3, LEVEL_SHAPES[3])):
         for ref in (one.b, one.v, one.u):
@@ -234,7 +239,12 @@
     each(0, 4, restrict_0(lambda p: l0.b[3 + p, pl.ds(O0, 32), :], store_b1))
     load_f.wait()
 
-    pl.semaphore_wait(barrier, 61 + 23)
+    pl.semaphore_wait(barrier, len(greeted))
+
+    def pass_on(n, targets):
+        for target in targets:
+            pl.semaphore_signal(ready.at[n], inc=1, device_id=target, device_id_type=MESH)
+
 
     def cut(d, first, size, width):
         if d == 0:
@@ -267,6 +277,11 @@
     send_near(0, l0.b, (3, 16), (O0, 32), 3, 3)
     send_near(1, l0.f, (3, 16), (O0, 32), 2, 2)
     send_near(2, l1.b, (3, 4), (O1, 16), 2, 4)
+    pass_on(
+        0,
+        [device(dg, dq) for dg in (-2, 2) for dq in (-1, 0, 1)]
+        + [device_xz(0, dz) for dz in (3, -3)],
+    )
 
     def clear(ref, blocks, rows, total_blocks, block_width, row_width):
         first, count = blocks
@@ -322,11 +337,14 @@
             )
             copy.start()
 
+    pl.semaphore_wait(ready.at[0], 8)
+
     def b2_parts(dq):
         src, dst, n = {0: (8, O2, 8), 1: (7, O2 - 9, 9), -1: (8, O2 + 8, 9)}[dq]
         return b2_own.at[pl.ds(src, n)], l2.b.at[1 + g, pl.ds(dst, n)]
 
     send_wide(4, b2_parts)
+    pass_on(1, [device_xz(dx, dz) for dx in range(4) for dz in (3, -3)])
     l2.b[1 + g, pl.ds(O2, 8), :] = b2_own[pl.ds(8, 8), :]
     each(1, 9, l1.weigh)
     arrive(3)
@@ -377,6 +395,7 @@
 
     gathered[pl.ds(2 * q, 1), :] = f4
     gathered[pl.ds(2 * q + 1, 1), :] = b4
+    pl.semaphore_wait(ready.at[1], 8)
     for d in far:
         here = gathered.at[pl.ds(2 * q, 2)]
         copy = pltpu.make_async_remote_copy(
@@ -395,10 +414,9 @@
     lane = lanes_of(NQ)
     row = lax.broadcasted_iota(jnp.int32, (NQ, 128), 0)
     odd = (lane & 1) == 1
-    plane = (lane // 2) & 7
     edges = (
-        plane == 7,
-        plane == 0,
+        (lane & 14) == 14,
+        (lane & 14) == 0,
         (row == NQ - 1) & odd,
         (row == 0) & jnp.logical_not(odd),
         lane >= 112,
@@ -525,6 +543,7 @@
         pltpu.SemaphoreType.DMA((2,)),
         pltpu.SemaphoreType.DMA((7,)),
         pltpu.SemaphoreType.DMA((7,)),
+        pltpu.SemaphoreType.REGULAR((2,)),
     ]
     return pl.pallas_call(
         kernel,
@@ -533,10 +552,10 @@
         out_specs=pl.BlockSpec(memory_space=pltpu.VMEM),
         scratch_shapes=scratch,
         compiler_params=pltpu.CompilerParams(
-            collective_id=0, has_side_effects=True, vmem_limit_bytes=60 * 2**20
+            collective_id=0, has_side_effects=True, vmem_limit_bytes=24 * 2**20
         ),
         cost_estimate=pl.CostEstimate(flops=10_000_000, bytes_accessed=3 * 262144, transcendentals=0),
-    )(right_side, coefficient)
+    )(pltpu.with_memory_space_constraint(right_side, pltpu.HBM), pltpu.with_memory_space_constraint(coefficient, pltpu.HBM))
 
 
 def solution(mesh):

time: 47 us -> 42.1 us (0.90)
  Pallas kernels: 45.2 us -> 41.3 us
  local copies, waits for them, and re-layouts: 1.67 us -> 0.71 us
    pallas_call x1, Pallas kernels: 45.2 us -> 41.3 us  [per_device(): pl.pallas_call(kernel, out_shape=jax.ShapeDtypeStruct((16, 32, 128), F32)...]
    unnamed x1, local copies, waits for them, and re-layouts: 1.67 us -> 0.71 us
where the time goes in v3:
time: 42.1 us; the launch traced here: 42 us
  Pallas kernels  41.3 us (98%)
  local copies, waits for them, and re-layouts  0.71 us (2%)
    pallas_call x1, Pallas kernels, per_device(): pl.pallas_call(kernel, out_shape=jax.ShapeDtypeStruct((16, 32, 128), F32)...  41.3 us

profile of v3, /device:TPU:1, one launch (start us, length us, event | category | flops | bytes accessed | tf_op | source)
XLA Modules:
  0.0 42.0 jit_solution(7549247006142012201)
XLA Ops:
  0.0 41.3 %shard_map.28 = f32[16,32,128]{2,1,0:T(8,128)S(1)} custom-call(f32[16,32,128]{2,1,0:T(8,128)} %f_hbm.1, f32[16,32,128]{2,1,0:T(8,128)} %b_hbm.1), custom_call_target="tpu_custom_call" | custom-call | flops 10000000 | bytes 786432 | tf_op jit(solution)/shard_map/pallas_call | solution.py:548
  41.3 0.7 %copy.4 = f32[16,32,128]{2,1,0:T(8,128)} copy(f32[16,32,128]{2,1,0:T(8,128)S(1)} %shard_map.28) | data formatting | bytes 524288

commit v4 on v3

--- a/solution.py
+++ b/solution.py
@@ -1,3 +1,5 @@
+import copy as copies
+
 import jax
 import jax.numpy as jnp
 from jax import lax
@@ -21,19 +23,29 @@
     return lax.broadcasted_iota(jnp.int32, (rows, 128), 1)
 
 
+def pick(v, index):
+    return jnp.take_along_axis(v, index, axis=1)
+
+
 def swap(v, bit):
     lane = lanes_of(v.shape[0])
     return jnp.where((lane & bit) == 0, roll(v, -bit), roll(v, bit))
 
 
 class Level:
-    def __init__(self, scale, rows, start, count, unit, planes, depth, pieces):
+    def __init__(self, scale, rows, start, unit, planes, depth, extent):
         self.half = 0.5 * scale
         self.rows = rows
         self.start = start
         self.unit = unit
         self.planes = planes
         self.depth = depth
+        self.extent = extent
+
+    def window(self, start, rows):
+        other = copies.copy(self)
+        other.start, other.rows = start, rows
+        return other
 
     def load(self, ref, i, shift=0):
         return ref[i, pl.ds(self.start + shift, self.rows), :]
@@ -49,15 +61,15 @@
             s = self.unit
             bits = (self.planes - 1) * s
             field = lanes_of(self.rows) & bits
-            xp = jnp.where(field != bits, roll(c, -s), roll(self.load(ref, i + 1), bits))
-            xm = jnp.where(field != 0, roll(c, s), roll(self.load(ref, i - 1), -bits))
+            xp = roll(jnp.where(field != 0, c, self.load(ref, i + 1)), -s)
+            xm = roll(jnp.where(field != bits, c, self.load(ref, i - 1)), s)
         yp, ym = self.load(ref, i, 1), self.load(ref, i, -1)
         zp, zm = roll(c, -self.depth), roll(c, self.depth)
         return c, (xp, xm, yp, ym, zp, zm)
 
     def weigh(self, i):
-        lane = lanes_of(self.rows)
-        first, last = lane < self.depth, lane >= 128 - self.depth
+        along = lanes_of(self.rows) & self.extent
+        first, last = along == 0, along == self.extent
         c, others = self.shifted(self.b, i)
         total = None
         for k, other in enumerate(others):
@@ -115,7 +127,7 @@
 
 LEVEL_SHAPES = ((22, R0), (10, R1), (10, R2), (10, R3))
 
-GROUP_ROWS = ((6, 54), (13, 16), (16, 8), (16, 8), (5, 40), (4, 46), (3, 42))
+GROUP_ROWS = ((6, 54), (13, 16), (16, 8), (16, 8), (5, 40), (4, 46), (3, 5), (3, 21), (3, 16))
 
 
 def kernel(f_hbm, b_hbm, out, *refs):
@@ -127,14 +139,14 @@
         return got
 
     lv = [
-        Level(1.0, 40, 8, 16, 1, 1, 1, 1),
-        Level(0.25, 24, 8, 4, 1, 2, 2, 1),
-        Level(0.0625, 24, 8, 8, 1, 4, 4, 1),
-        Level(0.015625, 16, 8, 8, 2, 2, 8, 1),
+        Level(1.0, 40, 8, 0, 1, 1, 127),
+        Level(0.25, 24, 8, 64, 2, 1, 63),
+        Level(0.0625, 24, 8, 32, 4, 1, 31),
+        Level(0.015625, 16, 8, 64, 2, 2, 30),
     ]
     for one in lv:
         one.b, one.f, one.v, one.u, one.d, one.inv, one.w = take(7)
-    pair, b2_own, f2_own, gathered, e_pad = take(5)
+    pair, b2_own, f2_own, all_b4, all_f4, e_pad = take(6)
     load_sem, send_sem, recv_sem, ready = take(4)
     l0, l1, l2, l3 = lv
 
@@ -146,7 +158,7 @@
     load_f.start()
 
     def device(dg, dq):
-        return {"gx": lax.rem(g + dg + NG, NG), "yz": lax.rem(q + dq + NQ, NQ)}
+        return {"gx": g + dg & NG - 1, "yz": q + dq & NQ - 1}
 
     near = [(dg, dq) for dg in (-1, 1) for dq in (-1, 1)] + [(0, -1), (0, 1), (-1, 0), (1, 0)]
     wide = [(dg, dq) for dg in (4, 3, 5, 2, 6, 1, 7, 0) for dq in (-1, 1, 0) if dg or dq]
@@ -185,7 +197,8 @@
     e_pad[pl.ds(0, 8), :] = jnp.zeros((8, 128), F32)
     e_pad[pl.ds(72, 8), :] = jnp.zeros((8, 128), F32)
 
-    even = (lanes_of(16) & 1) == 0
+    low = lanes_of(16) < 64
+    pairs = 2 * (lanes_of(16) & 63)
 
     def restrict_0(make, store):
         def body(i):
@@ -194,28 +207,31 @@
                 slot = 2 * i + half
                 pair[slot, pl.ds(0, 32), :] = make(2 * slot) + make(2 * slot + 1)
                 t = pair[slot, pl.ds(0, 16, stride=2), :] + pair[slot, pl.ds(1, 16, stride=2), :]
-                halves.append(t + swap(t, 1))
-            store(i, 0.125 * jnp.where(even, halves[0], halves[1]))
+                halves.append(pick(t, pairs) + pick(t, pairs + 1))
+            store(i, 0.125 * jnp.where(low, halves[0], halves[1]))
 
         return body
 
     def restrict_1(make, rows):
         lane = lanes_of(rows)
-        packed = None
+        parts = []
         for i in range(4):
             pair[i, pl.ds(0, 2 * rows), :] = make(i)
             t = pair[i, pl.ds(0, rows, stride=2), :] + pair[i, pl.ds(1, rows, stride=2), :]
-            t = t + swap(t, 1)
-            t = t + swap(t, 2)
-            packed = t if packed is None else jnp.where((lane & 3) == i, t, packed)
-        return 0.125 * packed
+            parts.append(t + roll(t, 64))
+        index = 2 * (lane & 31) + ((lane & 32) * 2)
+        halves = []
+        for i in (0, 2):
+            t = jnp.where(lane < 64, parts[i], parts[i + 1])
+            halves.append(pick(t, index) + pick(t, index + 1))
+        return 0.125 * jnp.where(lane < 64, halves[0], halves[1])
 
     def restrict_2(make):
         def one(i):
             pair[i, pl.ds(0, 24), :] = make(i)
             t = pair[i, pl.ds(0, 12, stride=2), :] + pair[i, pl.ds(1, 12, stride=2), :]
-            t = t + swap(t, 1)
-            return 0.125 * (t + swap(t, 4))
+            t = t + swap(t, 32)
+            return 0.125 * (t + swap(t, 1))
 
         return one
 
@@ -225,8 +241,8 @@
         for i in range(8):
             pair[i, pl.ds(0, 4), :] = make(i)
             t = pair[i, pl.ds(0, 2, stride=2), :] + pair[i, pl.ds(1, 2, stride=2), :]
-            t = t + swap(t, 2)
-            t = 0.125 * (t + swap(t, 8))
+            t = t + roll(t, 64)
+            t = 0.125 * pick(t + swap(t, 2), (lanes_of(2) >> 4) * 4)
             for j in range(2):
                 row = t[j : j + 1] if row is None else jnp.where(k == 2 * i + j, t[j : j + 1], row)
         return row
@@ -236,8 +252,24 @@
     def store_b1(i, v):
         l1.b[3 + i, pl.ds(O1, 16), :] = v
 
-    each(0, 4, restrict_0(lambda p: l0.b[3 + p, pl.ds(O0, 32), :], store_b1))
+    each(0, 4, restrict_0(lambda p: l0.b[3 + p, pl.ds(O0, 32), :], store_b1), 2)
     load_f.wait()
+
+    core = l0.window(14, 28)
+    each(4, 18, core.weigh, 7)
+    each(4, 18, core.first, 7)
+    core = l0.window(16, 24)
+    each(5, 17, lambda i: core.store(l0.u, i, core.smooth(l0.v, i)), 6)
+    rims = (l0.window(8, 8), l0.window(40, 8))
+
+    def outside(lo, width, hi, work):
+        def rim(i):
+            for one in rims:
+                work(one, i)
+
+        each(lo + width, hi - width, rim, (hi - lo - 2 * width) // 2)
+        for i in list(range(lo, lo + width)) + list(range(hi - width, hi)):
+            work(l0, i)
 
     pl.semaphore_wait(barrier, len(greeted))
 
@@ -309,15 +341,15 @@
 
     arrive(0)
     clear(l0.b, (3, 16), (O0, 32), 22, 3, 3)
-    each(1, 21, l0.weigh, 10)
+    outside(1, 3, 21, lambda one, i: one.weigh(i))
     arrive(1)
-    each(1, 21, l0.first, 10)
-    each(2, 20, lambda i: l0.store(l0.u, i, l0.smooth(l0.v, i)), 9)
+    outside(1, 3, 21, lambda one, i: one.first(i))
+    outside(2, 3, 20, lambda one, i: one.store(l0.u, i, one.smooth(l0.v, i)))
 
     def store_f1(i, v):
         l1.f[3 + i, pl.ds(O1, 16), :] = v
 
-    each(0, 4, restrict_0(lambda p: l0.residual(3 + p)[O0 - 8 : O0 - 8 + 32], store_f1))
+    each(0, 4, restrict_0(lambda p: l0.residual(3 + p)[O0 - 8 : O0 - 8 + 32], store_f1), 2)
     send_near(3, l1.f, (3, 4), (O1, 16), 2, 4)
 
     arrive(2)
@@ -346,7 +378,7 @@
     send_wide(4, b2_parts)
     pass_on(1, [device_xz(dx, dz) for dx in range(4) for dz in (3, -3)])
     l2.b[1 + g, pl.ds(O2, 8), :] = b2_own[pl.ds(8, 8), :]
-    each(1, 9, l1.weigh)
+    each(1, 9, l1.weigh, 4)
     arrive(3)
     each(1, 9, l1.first)
     each(2, 8, lambda i: l1.store(l1.u, i, l1.smooth(l1.v, i)))
@@ -370,15 +402,32 @@
         for i in range(1, 9):
             l2.b[i, pl.ds(O2 + 8, 9), :] = jnp.zeros((9, 128), F32)
 
-    each(1, 9, l2.weigh)
+    each(1, 9, l2.weigh, 4)
     b3_of = restrict_2(lambda i: l2.load(l2.b, i))
 
     def store_b3(i):
         l3.b[i, pl.ds(O3 - 4, 12), :] = b3_of(i)
 
     each(1, 9, store_b3)
-    each(1, 9, l3.weigh)
+    each(1, 9, l3.weigh, 4)
+
+    def send_rows(slot, ref, start, count, targets):
+        here = ref.at[pl.ds(start, count)]
+        for target in targets:
+            copy = pltpu.make_async_remote_copy(
+                src_ref=here,
+                dst_ref=here,
+                send_sem=send_sem.at[slot],
+                recv_sem=recv_sem.at[slot],
+                device_id=target,
+                device_id_type=MESH,
+            )
+            copy.start()
+
     b4 = restrict_3(lambda i: l3.b[1 + i, pl.ds(O3, 4), :])
+    pl.semaphore_wait(ready.at[1], 8)
+    all_b4[pl.ds(q, 1), :] = b4
+    send_rows(6, all_b4, q, 1, [device_xz(0, dz) for dz in (8, 7, 9, 6, 10, 5, 11, 4, 12, 3, 13, 2, 14, 1, 15)])
 
     arrive(5)
     each(1, 9, l2.first)
@@ -393,24 +442,12 @@
     each(1, 9, lambda i: l3.store(l3.u, i, l3.smooth(l3.v, i)))
     f4 = restrict_3(lambda i: l3.residual(1 + i)[O3 - 8 : O3 - 8 + 4])
 
-    gathered[pl.ds(2 * q, 1), :] = f4
-    gathered[pl.ds(2 * q + 1, 1), :] = b4
-    pl.semaphore_wait(ready.at[1], 8)
-    for d in far:
-        here = gathered.at[pl.ds(2 * q, 2)]
-        copy = pltpu.make_async_remote_copy(
-            src_ref=here,
-            dst_ref=here,
-            send_sem=send_sem.at[6],
-            recv_sem=recv_sem.at[6],
-            device_id=device(0, d),
-            device_id_type=MESH,
-        )
-        copy.start()
+    all_f4[pl.ds(q, 1), :] = f4
+    send_rows(7, all_f4, q, 1, [device(0, d) for d in far])
     arrive(6)
-
-    source = gathered[pl.ds(0, NQ, stride=2), :]
-    weight = gathered[pl.ds(1, NQ, stride=2), :]
+    send_rows(8, all_b4, pl.multiple_of((q >> 4) * 16, 16), 16, [device_xz(dx, 0) for dx in (2, 1, 3)])
+    arrive(8)
+    weight = all_b4[...]
     lane = lanes_of(NQ)
     row = lax.broadcasted_iota(jnp.int32, (NQ, 128), 0)
     odd = (lane & 1) == 1
@@ -437,6 +474,9 @@
         bottom_d = w if bottom_d is None else bottom_d + w
         bottom_w.append(jnp.where(edge, 0.0, w))
 
+    arrive(7)
+    source = all_f4[...]
+
     def apply_op(v):
         result = bottom_d * v
         for w, other in zip(bottom_w, bottom_shifts(v)):
@@ -451,23 +491,21 @@
     direction = source
     applied = None
     rho = total(source * source)
-    rho_prev = rho
-    alpha = omega = None
+    alpha = omega = shadow_bent = None
     for turn in range(BITERS):
         if turn > 0:
-            beta = (rho / rho_prev) * (alpha / omega)
+            beta = -(alpha * shadow_bent) / rho
+            rho = -(omega * shadow_bent)
             direction = residual + beta * (direction - omega * applied)
         applied = apply_op(direction)
         alpha = rho / total(source * applied)
         middle = residual - alpha * applied
         bent = apply_op(middle)
         omega = total(bent * middle) / total(bent * bent)
+        shadow_bent = total(source * bent)
         step = alpha * direction + omega * middle
         answer = step if answer is None else answer + step
         residual = middle - omega * bent
-        if turn + 1 < BITERS:
-            rho_prev = rho
-            rho = total(source * residual)
 
     e_pad[pl.ds(8, NQ), :] = answer
     fine = lax.broadcasted_iota(jnp.int32, (16, 128), 0) - 8
@@ -477,10 +515,7 @@
         jnp.where(fine < 4, e_pad[pl.ds(8 + q, 1), :], e_pad[pl.ds(9 + q, 1), :]),
     )
     parity = jnp.where((fine < 0) | ((fine >= 2) & (fine < 4)), 1, 0)
-    group = lanes_of(16) & ~15
-
-    def pick(v, index):
-        return jnp.take_along_axis(v, index, axis=1)
+    group = ((lanes_of(16) >> 2) & 7) * 16
 
     def up_3(i):
         wide_e = pick(near_rows, group + parity + 2 * (i - 1))
@@ -499,20 +534,20 @@
     each(1, 9, up_3s)
     each(1, 9, lambda i: l2.store(l2.u, i, l2.smooth(l2.v, i)))
 
-    spread = lanes_of(12) & ~3
+    spread = (lanes_of(12) & 63) >> 1
     for i in range(-1, 5):
         from_block = 1 + g + (i // 4)
-        v = pick(l2.u[from_block, pl.ds(O2 - 2, 12), :], spread + (i % 4))
+        v = pick(l2.u[from_block, pl.ds(O2 - 2, 12), :], spread + 32 * (i % 4))
         for k in range(2):
             pair[i + 1, pl.ds(k, 12, stride=2), :] = v
         l1.v[3 + i, pl.ds(O1 - 4, 24), :] = l1.u[3 + i, pl.ds(O1 - 4, 24), :] + pair[i + 1, pl.ds(0, 24), :]
     for i in range(-1, 5):
         l1.store(l1.u, 3 + i, l1.smooth(l1.v, 3 + i))
 
-    even20 = (lanes_of(20) & 1) == 0
+    spread = lanes_of(20) >> 1
     for i in range(-1, 9):
         v = l1.u[3 + (i // 2), pl.ds(O1 - 2, 20), :]
-        v = jnp.where(even20, v, roll(v, 1)) if i % 2 == 0 else jnp.where(even20, roll(v, -1), v)
+        v = pick(v, spread + 64 * (i % 2))
         for k in range(2):
             pair[i + 1, pl.ds(k, 20, stride=2), :] = v
         wide_v = pair[i + 1, pl.ds(0, 40), :]
@@ -538,11 +573,12 @@
         pltpu.VMEM((16, 48, 128), F32),
         pltpu.VMEM((24, 128), F32),
         pltpu.VMEM((8, 128), F32),
-        pltpu.VMEM((2 * NQ, 128), F32),
+        pltpu.VMEM((NQ, 128), F32),
+        pltpu.VMEM((NQ, 128), F32),
         pltpu.VMEM((80, 128), F32),
         pltpu.SemaphoreType.DMA((2,)),
-        pltpu.SemaphoreType.DMA((7,)),
-        pltpu.SemaphoreType.DMA((7,)),
+        pltpu.SemaphoreType.DMA((9,)),
+        pltpu.SemaphoreType.DMA((9,)),
         pltpu.SemaphoreType.REGULAR((2,)),
     ]
     return pl.pallas_call(

time: 42.1 us -> 41.5 us (0.986)
  Pallas kernels: 41.3 us -> 40.6 us
    pallas_call x1, Pallas kernels: 41.3 us -> 40.6 us  [per_device(): pl.pallas_call(kernel, out_shape=jax.ShapeDtypeStruct((16, 32, 128), F32)...]
where the time goes in v4:
time: 41.5 us; the launch traced here: 41.3 us
  Pallas kernels  40.6 us (98%)
  local copies, waits for them, and re-layouts  0.71 us (2%)
    pallas_call x1, Pallas kernels, per_device(): pl.pallas_call(kernel, out_shape=jax.ShapeDtypeStruct((16, 32, 128), F32)...  40.6 us

profile of v4, /device:TPU:1, one launch (start us, length us, event | category | flops | bytes accessed | tf_op | source)
XLA Modules:
  0.0 41.3 jit_solution(1861427555245516562)
XLA Ops:
  0.0 40.6 %shard_map.28 = f32[16,32,128]{2,1,0:T(8,128)S(1)} custom-call(f32[16,32,128]{2,1,0:T(8,128)} %f_hbm.1, f32[16,32,128]{2,1,0:T(8,128)} %b_hbm.1), custom_call_target="tpu_custom_call" | custom-call | flops 10000000 | bytes 786432 | tf_op jit(solution)/shard_map/pallas_call | solution.py:584
  40.6 0.7 %copy.4 = f32[16,32,128]{2,1,0:T(8,128)} copy(f32[16,32,128]{2,1,0:T(8,128)S(1)} %shard_map.28) | data formatting | bytes 524288

commit v5 on v4

--- a/solution.py
+++ b/solution.py
@@ -249,27 +249,6 @@
 
     load_b.wait()
 
-    def store_b1(i, v):
-        l1.b[3 + i, pl.ds(O1, 16), :] = v
-
-    each(0, 4, restrict_0(lambda p: l0.b[3 + p, pl.ds(O0, 32), :], store_b1), 2)
-    load_f.wait()
-
-    core = l0.window(14, 28)
-    each(4, 18, core.weigh, 7)
-    each(4, 18, core.first, 7)
-    core = l0.window(16, 24)
-    each(5, 17, lambda i: core.store(l0.u, i, core.smooth(l0.v, i)), 6)
-    rims = (l0.window(8, 8), l0.window(40, 8))
-
-    def outside(lo, width, hi, work):
-        def rim(i):
-            for one in rims:
-                work(one, i)
-
-        each(lo + width, hi - width, rim, (hi - lo - 2 * width) // 2)
-        for i in list(range(lo, lo + width)) + list(range(hi - width, hi)):
-            work(l0, i)
 
     pl.semaphore_wait(barrier, len(greeted))
 
@@ -307,8 +286,8 @@
         all_of(recv_sem.at[group], GROUP_ROWS[group]).wait()
 
     send_near(0, l0.b, (3, 16), (O0, 32), 3, 3)
+    load_f.wait()
     send_near(1, l0.f, (3, 16), (O0, 32), 2, 2)
-    send_near(2, l1.b, (3, 4), (O1, 16), 2, 4)
     pass_on(
         0,
         [device(dg, dq) for dg in (-2, 2) for dq in (-1, 0, 1)]
@@ -338,6 +317,28 @@
         def _():
             for i in range(first - block_width, first + count + block_width):
                 ref[i, pl.ds(start + height, row_width), :] = jnp.zeros((row_width, 128), F32)
+
+    def store_b1(i, v):
+        l1.b[3 + i, pl.ds(O1, 16), :] = v
+
+    each(0, 4, restrict_0(lambda p: l0.b[3 + p, pl.ds(O0, 32), :], store_b1), 2)
+    send_near(2, l1.b, (3, 4), (O1, 16), 2, 4)
+
+    core = l0.window(14, 28)
+    each(4, 18, core.weigh, 7)
+    each(4, 18, core.first, 7)
+    core = l0.window(16, 24)
+    each(5, 17, lambda i: core.store(l0.u, i, core.smooth(l0.v, i)), 6)
+    rims = (l0.window(8, 8), l0.window(40, 8))
+
+    def outside(lo, width, hi, work):
+        def rim(i):
+            for one in rims:
+                work(one, i)
+
+        each(lo + width, hi - width, rim, (hi - lo - 2 * width) // 2)
+        for i in list(range(lo, lo + width)) + list(range(hi - width, hi)):
+            work(l0, i)
 
     arrive(0)
     clear(l0.b, (3, 16), (O0, 32), 22, 3, 3)
@@ -378,7 +379,7 @@
     send_wide(4, b2_parts)
     pass_on(1, [device_xz(dx, dz) for dx in range(4) for dz in (3, -3)])
     l2.b[1 + g, pl.ds(O2, 8), :] = b2_own[pl.ds(8, 8), :]
-    each(1, 9, l1.weigh, 4)
+    each(1, 9, l1.weigh)
     arrive(3)
     each(1, 9, l1.first)
     each(2, 8, lambda i: l1.store(l1.u, i, l1.smooth(l1.v, i)))
@@ -402,14 +403,14 @@
         for i in range(1, 9):
             l2.b[i, pl.ds(O2 + 8, 9), :] = jnp.zeros((9, 128), F32)
 
-    each(1, 9, l2.weigh, 4)
+    each(1, 9, l2.weigh)
     b3_of = restrict_2(lambda i: l2.load(l2.b, i))
 
     def store_b3(i):
         l3.b[i, pl.ds(O3 - 4, 12), :] = b3_of(i)
 
     each(1, 9, store_b3)
-    each(1, 9, l3.weigh, 4)
+    each(1, 9, l3.weigh)
 
     def send_rows(slot, ref, start, count, targets):
         here = ref.at[pl.ds(start, count)]

time: 41.5 us -> 41.5 us (level)
  no operation moved by 1% of the time
where the time goes in v5:
time: 41.5 us; the launch traced here: 41.3 us
  Pallas kernels  40.6 us (98%)
  local copies, waits for them, and re-layouts  0.71 us (2%)
    pallas_call x1, Pallas kernels, per_device(): pl.pallas_call(kernel, out_shape=jax.ShapeDtypeStruct((16, 32, 128), F32)...  40.6 us

profile of v5, /device:TPU:1, one launch (start us, length us, event | category | flops | bytes accessed | tf_op | source)
XLA Modules:
  0.0 41.3 jit_solution(7105479621167228044)
XLA Ops:
  0.0 40.6 %shard_map.28 = f32[16,32,128]{2,1,0:T(8,128)S(1)} custom-call(f32[16,32,128]{2,1,0:T(8,128)} %f_hbm.1, f32[16,32,128]{2,1,0:T(8,128)} %b_hbm.1), custom_call_target="tpu_custom_call" | custom-call | flops 10000000 | bytes 786432 | tf_op jit(solution)/shard_map/pallas_call | solution.py:585
  40.6 0.7 %copy.4 = f32[16,32,128]{2,1,0:T(8,128)} copy(f32[16,32,128]{2,1,0:T(8,128)S(1)} %shard_map.28) | data formatting | bytes 524288

commit v6 on v5

--- a/solution.py
+++ b/solution.py
@@ -25,11 +25,6 @@
 
 def pick(v, index):
     return jnp.take_along_axis(v, index, axis=1)
-
-
-def swap(v, bit):
-    lane = lanes_of(v.shape[0])
-    return jnp.where((lane & bit) == 0, roll(v, -bit), roll(v, bit))
 
 
 class Level:
@@ -230,8 +225,9 @@
         def one(i):
             pair[i, pl.ds(0, 24), :] = make(i)
             t = pair[i, pl.ds(0, 12, stride=2), :] + pair[i, pl.ds(1, 12, stride=2), :]
-            t = t + swap(t, 32)
-            return 0.125 * (t + swap(t, 1))
+            t = t + roll(t, -32)
+            t = t + roll(t, -1)
+            return 0.125 * pick(t, lanes_of(12) & ~33)
 
         return one
 
@@ -242,7 +238,7 @@
             pair[i, pl.ds(0, 4), :] = make(i)
             t = pair[i, pl.ds(0, 2, stride=2), :] + pair[i, pl.ds(1, 2, stride=2), :]
             t = t + roll(t, 64)
-            t = 0.125 * pick(t + swap(t, 2), (lanes_of(2) >> 4) * 4)
+            t = 0.125 * pick(t + roll(t, -2), (lanes_of(2) >> 4) * 4)
             for j in range(2):
                 row = t[j : j + 1] if row is None else jnp.where(k == 2 * i + j, t[j : j + 1], row)
         return row

time: 41.5 us -> 41.5 us (level)
  no operation moved by 1% of the time
where the time goes in v6:
time: 41.5 us; the launch traced here: 41.4 us
  Pallas kernels  40.7 us (98%)
  local copies, waits for them, and re-layouts  0.71 us (2%)
    pallas_call x1, Pallas kernels, per_device(): pl.pallas_call(kernel, out_shape=jax.ShapeDtypeStruct((16, 32, 128), F32)...  40.7 us

profile of v6, /device:TPU:1, one launch (start us, length us, event | category | flops | bytes accessed | tf_op | source)
XLA Modules:
  0.0 41.4 jit_solution(14679520153380149982)
XLA Ops:
  0.0 40.7 %shard_map.28 = f32[16,32,128]{2,1,0:T(8,128)S(1)} custom-call(f32[16,32,128]{2,1,0:T(8,128)} %f_hbm.1, f32[16,32,128]{2,1,0:T(8,128)} %b_hbm.1), custom_call_target="tpu_custom_call" | custom-call | flops 10000000 | bytes 786432 | tf_op jit(solution)/shard_map/pallas_call | solution.py:581
  40.7 0.7 %copy.4 = f32[16,32,128]{2,1,0:T(8,128)} copy(f32[16,32,128]{2,1,0:T(8,128)S(1)} %shard_map.28) | data formatting | bytes 524288
